TPU v7x, 32 devices: a whole 2x2x4 slice. The times are simulated.
32 devices in a mesh: lsec: 4 (over x, core), rsec: 4 (over z), ops: 2 (over y).
Axes of the slice: x: 2, y: 2, z: 4, core: 2. Of those that a mesh axis runs over, the one named last changes fastest.
Arguments:
- psi: bfloat16 [16, 16, 128, 128], P(('lsec', 'rsec')), may hold values from -6 to 6
- left_ops: bfloat16 [4, 16, 128, 128], P('ops', ('lsec', 'rsec')), may hold values from -0.5 to 0.5
- right_ops: bfloat16 [4, 16, 128, 128], P('ops', ('lsec', 'rsec')), may hold values from -0.25 to 0.25
- left_order: int32 [16], replicated, may hold values from 0 to 15, each once
- right_order: int32 [16], replicated, may hold values from 0 to 15, each once
- left_qn: int32 [16], replicated, may hold values from 0 to 2
- right_qn: int32 [16], replicated, may hold values from 0 to 2
- left_dims: int32 [16], replicated, may hold values from 96 to 128
- right_dims: int32 [16], replicated, may hold values from 96 to 128
Outputs:
- first_sigma: bfloat16 [16, 16, 128, 128], P(('lsec', 'rsec'))
- second_sigma: bfloat16 [16, 16, 128, 128], P(('lsec', 'rsec'), 'ops')
Inputs may be any that keep to these rules, and one draw needn't show every extreme that they name: left_order holds each left sector once. right_order holds each right sector once.
All inputs are finite; a program needn't handle non-finite values.
Results may differ from a plain program's by a relative error of at most 0.025.
Values may be sent and summed in bfloat16 or wider, within the bound.
A program may use at most 64 MiB of HBM per device.

v0:
```python
import jax
import jax.numpy as jnp
from jax import lax
from jax.sharding import PartitionSpec as P

SPREAD = 1


def relayout(blocks):
    return lax.all_to_all(blocks, ("lsec", "rsec"), split_axis=1, concat_axis=1, tiled=True)


def inverse(order):
    count = order.shape[0]
    return jnp.zeros((count,), jnp.int32).at[order].set(jnp.arange(count, dtype=jnp.int32))


def on_device(
    psi, left_ops, right_ops, left_order, right_order, left_qn, right_qn, left_dims, right_dims
):
    slot = lax.axis_index(("lsec", "rsec"))
    width = psi.shape[-1]
    line = jnp.arange(width, dtype=jnp.int32)
    left_sector = left_order[slot]
    right_sector = right_order[slot]
    inv_left = inverse(left_order)
    inv_right = inverse(right_order)
    left_here = left_ops[:, 0]
    right_here = right_ops[:, 0]
    allowed_row = jnp.abs(left_qn[left_sector] - right_qn) <= SPREAD
    row_used = line < left_dims[left_sector]
    col_used = line[None, :] < right_dims[:, None]
    mask_left = allowed_row[:, None, None] & row_used[None, :, None] & col_used[:, None, :]
    allowed_col = jnp.abs(left_qn - right_qn[right_sector]) <= SPREAD
    rows_used = line[None, :] < left_dims[:, None]
    cols_here = line < right_dims[right_sector]
    mask_right = allowed_col[:, None, None] & rows_used[:, :, None] & cols_here[None, None, :]
    start = jnp.where(mask_left, psi[0], jnp.zeros((), jnp.bfloat16))
    start_slots = start[right_order]
    lefted = jnp.einsum(
        "kxy,byz->kbxz", left_here, start_slots, preferred_element_type=jnp.float32
    ).astype(jnp.bfloat16)
    arrived = relayout(lefted)
    partial_value = jnp.einsum(
        "kixy,kzy->ixz", arrived, right_here, preferred_element_type=jnp.float32
    )
    partial_value = partial_value[inv_left]
    summed = lax.psum(partial_value.astype(jnp.bfloat16), "ops").astype(jnp.float32)
    first = jnp.where(mask_right, summed, 0.0).astype(jnp.bfloat16)
    first_slots = first[left_order]
    righted = jnp.einsum(
        "ixy,kzy->kixz", first_slots, right_here, preferred_element_type=jnp.float32
    ).astype(jnp.bfloat16)
    returned = relayout(righted)
    second_partial = jnp.einsum(
        "kxy,kjyz->jxz", left_here, returned, preferred_element_type=jnp.float32
    )
    second_partial = second_partial[inv_right]
    second_share = lax.psum_scatter(
        second_partial.astype(jnp.bfloat16), "ops", scatter_dimension=0, tiled=True
    ).astype(jnp.float32)
    count = second_share.shape[0]
    mask_second = lax.dynamic_slice_in_dim(mask_left, lax.axis_index("ops") * count, count, 0)
    second = jnp.where(mask_second, second_share, 0.0).astype(jnp.bfloat16)
    return (first[None], second[None])


def solution(mesh):
    placed = (
        P(("lsec", "rsec"), None, None, None),
        P("ops", ("lsec", "rsec"), None, None),
        P("ops", ("lsec", "rsec"), None, None),
        P(),
        P(),
        P(),
        P(),
        P(),
        P(),
    )
    return jax.shard_map(
        on_device,
        mesh=mesh,
        in_specs=placed,
        out_specs=(P(("lsec", "rsec"), None, None, None), P(("lsec", "rsec"), "ops", None, None)),
        check_vma=False,
    )
```

profile of v0, /device:TPU:0, one launch (start us, length us, event | category | flops | bytes accessed | tf_op | source)
XLA Modules:
  0.0 139.7 jit_solution(4243030337078179943)
XLA Ops:
  7.2 0.0 copy-start
  7.2 0.0 copy-start.3
  7.2 0.0 copy-start.8
  7.2 0.0 copy-start.5
  7.2 0.0 copy-start.6
  7.2 0.0 copy-start.4
  7.2 1.3 dynamic_slice.24
  9.8 1.3 copy.11
  11.8 0.0 copy-done.3
  11.8 0.6 dynamic_slice.26
  12.4 0.6 iota_compare_fusion.2
  13.1 0.0 copy-done.8
  13.1 0.6 dynamic_slice.25
  13.7 0.0 copy-done.5
  13.7 0.0 copy-done.6
  13.7 0.7 abs_compare_fusion
  14.3 0.0 copy-done.4
  14.4 0.1 iota_compare_fusion
  14.4 0.0 copy-start.2
  14.4 0.3 bitcast_select_fusion
  14.8 0.6 gather_fusion
  15.4 0.0 copy-done.2
  15.4 1.4 %fusion = bf16[2,16,128,128]{3,2,0,1:T(8,128)(2,1)} fusion(bf16[16,128,128]{1,2,0:T(8,128)(2,1)S(1)} %gather_fusion, bf16[2,1,128,128]{3,2,1,0:T(8,128)(2,1)S(1)} %copy-done.2), kind=kOutput, calls=%fused_computation.8 | convolution fusion | flops 134742016 | bytes 1638400 | tf_op jit(solution)/shard_map/kxy,byz->kbxz/dot_general | solution.py:40
  16.9 0.0 copy-start.7
  16.9 7.5 %all-to-all-start = ((bf16[2,16,128,128]{3,2,0,1:T(8,128)(2,1)}), bf16[2,16,128,128]{3,2,0,1:T(8,128)(2,1)S(1)}, u32[]{:S(2)}, u32[]{:S(2)}) async-start(bf16[2,16,128,128]{3,2,0,1:T(8,128)(2,1)} %fusion), calls=%async_computation | async-start | bytes 2097152 | tf_op jit(solution)/shard_map/all_to_all | solution.py:10
  24.4 0.0 all-reduce.2.cloned.1.call-start
  24.4 0.6 dynamic_slice.21
  26.9 0.6 dynamic_slice.23
  27.5 0.6 dynamic_slice.22
  28.1 0.0 copy-done.7
  28.1 0.6 scatter_custom_fusion
  28.8 22.6 %all-to-all-done = bf16[2,16,128,128]{3,2,0,1:T(8,128)(2,1)S(1)} async-done(((bf16[2,16,128,128]{3,2,0,1:T(8,128)(2,1)}), bf16[2,16,128,128]{3,2,0,1:T(8,128)(2,1)S(1)}, u32[]{:S(2)}, u32[]{:S(2)}) %all-to-all-start) | async-done | bytes 1048608 | tf_op jit(solution)/shard_map/all_to_all | solution.py:10
  51.3 0.0 copy-done
  51.3 0.4 convolution_bitcast_fusion.1
  51.8 1.4 %gather_fusion.1 = bf16[16,128,128]{2,1,0:T(8,128)(2,1)} fusion(bf16[16,128,128]{2,1,0:T(8,128)(2,1)S(1)} %convolution_bitcast_fusion.1, s32[1024]{0:T(1024)S(1)} %pad_clamp_fusion.2), kind=kCustom, calls=%fused_computation.1 | custom fusion | bytes 1048640 | tf_op jit(solution)/shard_map/gather | solution.py:47
  53.2 0.0 all-reduce.2.cloned.1.call-update
  53.2 0.7 iota_compare_fusion.3
  53.9 0.6 abs_compare_fusion.1
  54.4 0.1 fusion.9
  54.5 26.1 %all-reduce.2.cloned.1.call-done = bf16[16,128,128]{2,1,0:T(8,128)(2,1)} async-done(((bf16[16,128,128]{2,1,0:T(8,128)(2,1)}), bf16[16,128,128]{2,1,0:T(8,128)(2,1)}) %all-reduce.2.cloned.1.call-update) | async-done | bytes 524304 | tf_op jit(solution)/shard_map/psum | solution.py:48
  80.6 1.4 select_convert_fusion
  82.0 0.6 gather_fusion.2
  82.6 1.4 %fusion.1 = bf16[2,16,128,128]{2,3,0,1:T(8,128)(2,1)} fusion(bf16[16,128,128]{2,1,0:T(8,128)(2,1)S(1)} %gather_fusion.2, bf16[2,1,128,128]{3,2,1,0:T(8,128)(2,1)S(1)} %copy-done), kind=kOutput, calls=%fused_computation.9 | convolution fusion | flops 134742016 | bytes 1638400 | tf_op jit(solution)/shard_map/ixy,kzy->kixz/dot_general | solution.py:51
  84.1 5.6 %all-to-all-start.1 = ((bf16[2,16,128,128]{2,3,0,1:T(8,128)(2,1)}), bf16[2,16,128,128]{2,3,0,1:T(8,128)(2,1)S(1)}, u32[]{:S(2)}, u32[]{:S(2)}) async-start(bf16[2,16,128,128]{2,3,0,1:T(8,128)(2,1)} %fusion.1), calls=%async_computation.1 | async-start | bytes 2097152 | tf_op jit(solution)/shard_map/all_to_all | solution.py:10
  89.7 0.0 reduce-scatter.2.cloned.1.call-start
  89.7 0.6 scatter_custom_fusion.1
  90.4 26.3 %all-to-all-done.1 = bf16[2,16,128,128]{2,3,0,1:T(8,128)(2,1)S(1)} async-done(((bf16[2,16,128,128]{2,3,0,1:T(8,128)(2,1)}), bf16[2,16,128,128]{2,3,0,1:T(8,128)(2,1)S(1)}, u32[]{:S(2)}, u32[]{:S(2)}) %all-to-all-start.1) | async-done | bytes 1048608 | tf_op jit(solution)/shard_map/all_to_all | solution.py:10
  116.6 0.4 convolution_bitcast_fusion
  117.1 0.0 copy-start.1
  117.1 1.4 %gather_fusion.3 = bf16[16,128,128]{1,2,0:T(8,128)(2,1)} fusion(bf16[16,128,128]{1,2,0:T(8,128)(2,1)S(1)} %convolution_bitcast_fusion, s32[1024]{0:T(1024)S(1)} %pad_clamp_fusion), kind=kCustom, calls=%fused_computation.3 | custom fusion | bytes 1048640 | tf_op jit(solution)/shard_map/gather | solution.py:58
  118.5 0.0 reduce-scatter.2.cloned.1.call-update
  118.5 0.3 broadcast_and_fusion
  118.9 0.0 copy-done.1
  118.9 1.1 fusion.16
  120.0 10.9 %reduce-scatter.2.cloned.1.call-done = bf16[8,128,128]{1,2,0:T(8,128)(2,1)} async-done(((bf16[16,128,128]{1,2,0:T(8,128)(2,1)}), bf16[8,128,128]{1,2,0:T(8,128)(2,1)}) %reduce-scatter.2.cloned.1.call-update) | async-done | bytes 262160 | tf_op jit(solution)/shard_map/reduce_scatter | solution.py:59
  130.9 1.0 fusion.4
  132.0 0.9 copy.12
  (10 shorter events, 0.0 us)
Async XLA Ops:
  7.2 44.2 %copy-start = (bf16[2,1,128,128]{3,2,1,0:T(8,128)(2,1)S(1)}, bf16[2,1,128,128]{3,2,1,0:T(8,128)(2,1)}, u32[]{:S(2)}) copy-start(bf16[2,1,128,128]{3,2,1,0:T(8,128)(2,1)} %param.11) | copy-start | bytes 196612
  7.2 4.6 %copy-start.3 = (s32[16]{0:T(128)S(1)}, s32[16]{0:T(128)}, u32[]{:S(2)}) copy-start(s32[16]{0:T(128)} %param.16) | copy-start | bytes 196
  7.2 5.9 %copy-start.8 = (s32[16]{0:T(128)S(1)}, s32[16]{0:T(128)}, u32[]{:S(2)}) copy-start(s32[16]{0:T(128)} %param.14) | copy-start | bytes 196
  7.2 6.5 %copy-start.5 = (s32[16]{0:T(128)S(1)}, s32[16]{0:T(128)}, u32[]{:S(2)}) copy-start(s32[16]{0:T(128)} %param.13) | copy-start | bytes 196
  7.2 6.5 %copy-start.6 = (s32[16]{0:T(128)S(1)}, s32[16]{0:T(128)}, u32[]{:S(2)}) copy-start(s32[16]{0:T(128)} %param.15) | copy-start | bytes 196
  7.2 7.1 %copy-start.4 = (s32[16]{0:T(128)S(1)}, s32[16]{0:T(128)}, u32[]{:S(2)}) copy-start(s32[16]{0:T(128)} %param.17) | copy-start | bytes 196
  14.4 1.0 copy-start.2
  16.9 11.2 %copy-start.7 = (s32[16]{0:T(128)S(1)}, s32[16]{0:T(128)}, u32[]{:S(2)}) copy-start(s32[16]{0:T(128)} %param.12) | copy-start | bytes 196
  16.9 34.5 %all-to-all-start = ((bf16[2,16,128,128]{3,2,0,1:T(8,128)(2,1)}), bf16[2,16,128,128]{3,2,0,1:T(8,128)(2,1)S(1)}, u32[]{:S(2)}, u32[]{:S(2)}) async-start(bf16[2,16,128,128]{3,2,0,1:T(8,128)(2,1)} %fusion), calls=%async_computation | async-start | bytes 2097152 | tf_op jit(solution)/shard_map/all_to_all | solution.py:10
  24.4 56.2 %all-reduce.2.cloned.1.call-start = ((), (), s32[]{:S(2)}) async-start(), calls=%async_computation.3 | async-start | bytes 1048576 | tf_op jit(solution)/shard_map/psum | solution.py:48
  84.1 32.6 %all-to-all-start.1 = ((bf16[2,16,128,128]{2,3,0,1:T(8,128)(2,1)}), bf16[2,16,128,128]{2,3,0,1:T(8,128)(2,1)S(1)}, u32[]{:S(2)}, u32[]{:S(2)}) async-start(bf16[2,16,128,128]{2,3,0,1:T(8,128)(2,1)} %fusion.1), calls=%async_computation.1 | async-start | bytes 2097152 | tf_op jit(solution)/shard_map/all_to_all | solution.py:10
  89.7 41.2 %reduce-scatter.2.cloned.1.call-start = ((), (), s32[]{:S(2)}) async-start(), calls=%async_computation.4 | async-start | bytes 786432 | tf_op jit(solution)/shard_map/reduce_scatter | solution.py:59
  117.1 1.8 %copy-start.1 = (bf16[16,128,128]{2,1,0:T(8,128)(2,1)S(1)}, bf16[16,128,128]{2,1,0:T(8,128)(2,1)}, u32[]{:S(2)}) copy-start(bf16[16,128,128]{2,1,0:T(8,128)(2,1)} %all-reduce.2.cloned.1.call-done) | copy-start | bytes 1572868
Sparse Core Ops, SparseCore 0:
  53.3 27.2 all-reduce.1
  118.6 12.2 reduce-scatter.1
where the time goes:
time: 140 us
  waiting for transfers between devices  85.9 us (61%)
  between operations  18.2 us (13%)
  starting transfers between devices  13.2 us (9%)
  local copies, waits for them, and re-layouts  11.8 us (8%)
  other arithmetic  6.93 us (5%)
  matrix products  3.69 us (3%)
    all_to_all x2, waiting for transfers between devices, relayout(): lax.all_to_all(blocks, ('lsec', 'rsec'), split_axis=1, concat_axis=1, til...  48.8 us
    psum x1, waiting for transfers between devices, on_device(): lax.psum(partial_value.astype(jnp.bfloat16), 'ops').astype(jnp.float32)  26.1 us
    all_to_all x2, starting transfers between devices, relayout(): lax.all_to_all(blocks, ('lsec', 'rsec'), split_axis=1, concat_axis=1, til...  13.1 us
    reduce_scatter x1, waiting for transfers between devices, on_device(): lax.psum_scatter(second_partial.astype(jnp.bfloat16), 'ops', scatter_dime...  10.9 us
  transfers between devices with their start and end apart: 4, of which 4 were waited for; matrix products, arithmetic and copies ran while one was open for 4% of the time, Pallas kernels for 0%

commit v1 on v0

--- a/solution.py
+++ b/solution.py
@@ -1,9 +1,16 @@
+import functools
+
 import jax
 import jax.numpy as jnp
 from jax import lax
+from jax.experimental import pallas as pl
+from jax.experimental.pallas import tpu as pltpu
 from jax.sharding import PartitionSpec as P
 
 SPREAD = 1
+VMEM_BUDGET = 24 * 2**20
+MESH = pl.DeviceIdType.MESH
+NT = (((1,), (1,)), ((), ()))
 
 
 def relayout(blocks):
@@ -15,7 +22,7 @@
     return jnp.zeros((count,), jnp.int32).at[order].set(jnp.arange(count, dtype=jnp.int32))
 
 
-def on_device(
+def by_collectives(
     psi, left_ops, right_ops, left_order, right_order, left_qn, right_qn, left_dims, right_dims
 ):
     slot = lax.axis_index(("lsec", "rsec"))
@@ -65,7 +72,301 @@
     return (first[None], second[None])
 
 
+def kernel(
+    nz,
+    nl,
+    psi_ref,
+    left_ref,
+    right_ref,
+    left_order,
+    right_order,
+    left_qn,
+    right_qn,
+    left_dims,
+    right_dims,
+    first_ref,
+    second_ref,
+    rbuf,
+    lbuf,
+    start,
+    terms,
+    sigma,
+    landed,
+    lsend,
+    lrecv,
+    zsend,
+    zrecv,
+    xsend,
+    xrecv,
+    ysend,
+    yrecv,
+    dsend,
+    drecv,
+    csend,
+    crecv,
+    ssend,
+    srecv,
+):
+    l = lax.axis_index("lsec")
+    z = lax.axis_index("rsec")
+    o = lax.axis_index("ops")
+    xp = (l + 2) % nl
+    cp = l + 1 - 2 * (l % 2)
+    op = 1 - o
+    me = l * nz + z
+    slots = nl * nz
+    width = psi_ref.shape[-1]
+    kdev = left_ref.shape[0]
+    to_y = {"ops": op}
+    to_x = {"lsec": xp}
+    to_c = {"lsec": cp}
+    sent = []
+
+    def send(src, dst, send_sem, recv_sem, where):
+        copy = pltpu.make_async_remote_copy(
+            src_ref=src,
+            dst_ref=dst,
+            send_sem=send_sem,
+            recv_sem=recv_sem,
+            device_id=where,
+            device_id_type=MESH,
+        )
+        copy.start()
+        sent.append(copy)
+
+    def arrive(ref, sem):
+        pltpu.make_async_copy(ref, ref, sem).wait()
+
+    rbuf[o, me] = right_ref[:, 0]
+    lbuf[o] = left_ref[:, 0]
+
+    barrier = pltpu.get_barrier_semaphore()
+    for s in range(nz):
+        for t in range(nl):
+            if s or t:
+                pl.semaphore_signal(
+                    barrier,
+                    inc=1,
+                    device_id={"lsec": (l + t) % nl, "rsec": (z + s) % nz},
+                    device_id_type=MESH,
+                )
+    pl.semaphore_signal(barrier, inc=1, device_id=to_y, device_id_type=MESH)
+    pl.semaphore_wait(barrier, slots)
+
+    def slot_of(lane, s):
+        return lane * nz + (z + s) % nz
+
+    send(lbuf.at[o], lbuf.at[o], lsend, lrecv, to_y)
+
+    def stage_one(s):
+        if s:
+            arrive(rbuf.at[o, slot_of(l, s)], zrecv.at[s])
+        piece = rbuf.at[o, slot_of(l, s)]
+        send(piece, piece, ysend.at[s], yrecv.at[s], to_y)
+        send(piece, piece, xsend.at[s], xrecv.at[s], to_x)
+        send(piece, piece, csend.at[0, s], crecv.at[0, s], to_c)
+
+    def stage_two(s):
+        from_x = rbuf.at[o, slot_of(xp, s)]
+        arrive(from_x, xrecv.at[s])
+        half = rbuf.at[o, slot_of(xp, s), 0]
+        send(half, half, dsend.at[0, s], drecv.at[0, s], to_y)
+        send(from_x, from_x, csend.at[1, s], crecv.at[1, s], to_c)
+        from_y = rbuf.at[op, slot_of(l, s)]
+        arrive(from_y, yrecv.at[s])
+        rest = rbuf.at[op, slot_of(l, s), pl.ds(1, kdev - 1)]
+        send(rest, rest, dsend.at[1, s], drecv.at[1, s], to_x)
+        send(from_y, from_y, csend.at[2, s], crecv.at[2, s], to_c)
+
+    def stage_three(s):
+        piece = rbuf.at[op, slot_of(xp, s)]
+        arrive(rbuf.at[op, slot_of(xp, s), 0], drecv.at[0, s])
+        arrive(rbuf.at[op, slot_of(xp, s), pl.ds(1, kdev - 1)], drecv.at[1, s])
+        send(piece, piece, csend.at[3, s], crecv.at[3, s], to_c)
+
+    def stage_four(s):
+        cx = (cp + 2) % nl
+        arrive(rbuf.at[o, slot_of(cp, s)], crecv.at[0, s])
+        arrive(rbuf.at[o, slot_of(cx, s)], crecv.at[1, s])
+        arrive(rbuf.at[op, slot_of(cp, s)], crecv.at[2, s])
+        arrive(rbuf.at[op, slot_of(cx, s)], crecv.at[3, s])
+
+    for s in range(1, nz):
+        piece = rbuf.at[o, me]
+        send(piece, piece, zsend.at[s], zrecv.at[s], {"rsec": (z + nz - s) % nz})
+    stage_one(0)
+
+    sector = left_order[me]
+    my_qn = left_qn[sector]
+    rows = lax.broadcasted_iota(jnp.int32, (width, width), 0)
+    cols = lax.broadcasted_iota(jnp.int32, (width, width), 1)
+    rows_used = rows < left_dims[sector]
+
+    def masked(value, b):
+        used = jnp.where(jnp.abs(my_qn - right_qn[b]) <= SPREAD, right_dims[b], 0)
+        return jnp.where(rows_used & (cols < used), value, 0.0).astype(jnp.bfloat16)
+
+    def left_terms(half, pair):
+        both = jnp.dot(
+            lbuf[half].reshape(kdev * width, width), start[pair], preferred_element_type=jnp.float32
+        ).astype(jnp.bfloat16)
+        both = both.reshape(kdev, width, 2 * width)
+        terms[2 * pair, half] = both[:, :, :width]
+        terms[2 * pair + 1, half] = both[:, :, width:]
+
+    def own_terms(pair, carry):
+        blocks = []
+        for j in (2 * pair, 2 * pair + 1):
+            b = right_order[j]
+            blocks.append(masked(psi_ref[0, b].astype(jnp.float32), b))
+        start[pair] = jnp.concatenate(blocks, axis=1)
+        left_terms(o, pair)
+        return carry
+
+    def other_terms(pair, carry):
+        left_terms(op, pair)
+        return carry
+
+    lax.fori_loop(0, slots // 2, own_terms, 0)
+    stage_one(1)
+    stage_two(0)
+    arrive(lbuf.at[op], lrecv)
+    lax.fori_loop(0, slots // 2, other_terms, 0)
+
+    def lanes(ref, j):
+        return jnp.concatenate([ref[j, h, k] for h in range(2) for k in range(kdev)], axis=1)
+
+    def right_lanes(j):
+        return jnp.concatenate([rbuf[h, j, k] for h in range(2) for k in range(kdev)], axis=1)
+
+    def first_blocks(s):
+        for t in range(nl):
+            j = slot_of((l + t) % nl, s)
+            value = lax.dot_general(
+                lanes(terms, j), right_lanes(j), NT, preferred_element_type=jnp.float32
+            )
+            sigma[j] = masked(value, right_order[j])
+        for t in range(nl):
+            j = slot_of((l + t) % nl, s)
+            if s or t:
+                send(
+                    sigma.at[j],
+                    landed.at[me],
+                    ssend.at[s, t],
+                    srecv.at[s, t],
+                    {"lsec": (l + t) % nl, "rsec": (z + s) % nz},
+                )
+            else:
+                landed[me] = sigma[j]
+
+    for step in range(2, nz + 3):
+        if step < nz:
+            stage_one(step)
+        if 1 <= step - 1 < nz:
+            stage_two(step - 1)
+        if 0 <= step - 2 < nz:
+            stage_three(step - 2)
+        if 0 <= step - 3 < nz:
+            stage_four(step - 3)
+            first_blocks(step - 3)
+
+    def slot_holding(order, wanted):
+        found = jnp.int32(0)
+        for j in range(slots):
+            found = jnp.where(order[j] == wanted, j, found)
+        return found
+
+    count = second_ref.shape[1]
+
+    def second_block(i, carry):
+        b = o * count + i
+        j = slot_holding(right_order, b)
+        state = sigma[j]
+        value = None
+        for h in range(2):
+            for k in range(kdev):
+                inner = lax.dot_general(
+                    state, rbuf[h, j, k], NT, preferred_element_type=jnp.float32
+                ).astype(jnp.bfloat16)
+                outer = jnp.dot(lbuf[h, k], inner, preferred_element_type=jnp.float32)
+                value = outer if value is None else value + outer
+        second_ref[0, i] = masked(value, b)
+        return carry
+
+    lax.fori_loop(0, count, second_block, 0, unroll=2)
+
+    for s in range(nz):
+        for t in range(nl):
+            if s or t:
+                source = ((l + nl - t) % nl) * nz + (z + nz - s) % nz
+                arrive(landed.at[source], srecv.at[s, t])
+
+    def place(a, carry):
+        first_ref[0, a] = landed[slot_holding(left_order, a)]
+        return carry
+
+    lax.fori_loop(0, slots, place, 0)
+
+    for copy in sent:
+        copy.wait_send()
+
+
+def by_kernel(nz, nl, psi, left_ops, right_ops, *tables):
+    slots = nl * nz
+    width = psi.shape[-1]
+    kdev = left_ops.shape[0]
+    block = (width, width)
+    dma = pltpu.SemaphoreType.DMA
+    bf16 = jnp.bfloat16
+    vmem = pl.BlockSpec(memory_space=pltpu.VMEM)
+    smem = pl.BlockSpec(memory_space=pltpu.SMEM)
+    flops = 2 * width**3 * 2 * kdev * slots * 3
+    return pl.pallas_call(
+        functools.partial(kernel, nz, nl),
+        out_shape=(
+            jax.ShapeDtypeStruct((1, slots) + block, bf16),
+            jax.ShapeDtypeStruct((1, slots // 2) + block, bf16),
+        ),
+        in_specs=[vmem] * 3 + [smem] * 6,
+        out_specs=(vmem, vmem),
+        scratch_shapes=[
+            pltpu.VMEM((2, slots, kdev) + block, bf16),
+            pltpu.VMEM((2, kdev) + block, bf16),
+            pltpu.VMEM((slots // 2, width, 2 * width), bf16),
+            pltpu.VMEM((slots, 2, kdev) + block, bf16),
+            pltpu.VMEM((slots,) + block, bf16),
+            pltpu.VMEM((slots,) + block, bf16),
+            dma,
+            dma,
+            dma((nz,)),
+            dma((nz,)),
+            dma((nz,)),
+            dma((nz,)),
+            dma((nz,)),
+            dma((nz,)),
+            dma((2, nz)),
+            dma((2, nz)),
+            dma((4, nz)),
+            dma((4, nz)),
+            dma((nz, nl)),
+            dma((nz, nl)),
+        ],
+        compiler_params=pltpu.CompilerParams(
+            collective_id=0, has_side_effects=True, vmem_limit_bytes=40 * 2**20
+        ),
+        cost_estimate=pl.CostEstimate(flops=flops, bytes_accessed=4 * 2**20, transcendentals=0),
+    )(psi, left_ops, right_ops, *tables)
+
+
 def solution(mesh):
+    nl, nz, no = mesh.shape["lsec"], mesh.shape["rsec"], mesh.shape["ops"]
+
+    def on_device(psi, left_ops, right_ops, *tables):
+        gathered = no * nl * nz * left_ops.size * left_ops.dtype.itemsize
+        if no == 2 and nl == 4 and left_ops.shape[0] > 1 and 3 * gathered <= VMEM_BUDGET:
+            return by_kernel(nz, nl, psi, left_ops, right_ops, *tables)
+        return by_collectives(psi, left_ops, right_ops, *tables)
+
     placed = (
         P(("lsec", "rsec"), None, None, None),
         P("ops", ("lsec", "rsec"), None, None),

time: 140 us -> 43.2 us (0.31)
  waiting for transfers between devices: 85.9 us -> 0 us
  Pallas kernels: 0 us -> 34.1 us
  between operations: 18.2 us -> 0.66 us
  starting transfers between devices: 13.2 us -> 0 us
  other arithmetic: 6.93 us -> 0 us
  matrix products: 3.69 us -> 0 us
  local copies, waits for them, and re-layouts: 11.8 us -> 8.14 us
    all_to_all x2 -> x0, waiting for transfers between devices: 48.8 us -> none  [relayout(): lax.all_to_all(blocks, ('lsec', 'rsec'), split_axis=1, concat_axis=1, til...]
    pallas_call x0 -> x1, Pallas kernels: none -> 34.1 us  [by_kernel(): pl.pallas_call(functools.partial(kernel, nz, nl), out_shape=(jax.ShapeDty...]
    psum x1 -> x0, waiting for transfers between devices: 26.1 us -> none  [on_device(): lax.psum(partial_value.astype(jnp.bfloat16), 'ops').astype(jnp.float32)]
    all_to_all x2 -> x0, starting transfers between devices: 13.1 us -> none  [relayout(): lax.all_to_all(blocks, ('lsec', 'rsec'), split_axis=1, concat_axis=1, til...]
    reduce_scatter x1 -> x0, waiting for transfers between devices: 10.9 us -> none  [on_device(): lax.psum_scatter(second_partial.astype(jnp.bfloat16), 'ops', scatter_dime...]
    unnamed x20, local copies, waits for them, and re-layouts: 2.21 us -> 8.14 us
    dynamic_slice x6 -> x0, local copies, waits for them, and re-layouts: 4.19 us -> none  [the longest x1 1.29 us: on_device(): left_sector = left_order[slot]]
    gather x4 -> x0, local copies, waits for them, and re-layouts: 4.11 us -> none  [the longest x1 1.41 us: on_device(): partial_value = partial_value[inv_left]]
  transfers between devices with their start and end apart: 4 -> 0, of which waited for: 4 -> 0; matrix products, arithmetic and copies ran while one was open for 4% -> 0% of each run, Pallas kernels for 0% -> 0%
where the time goes in v1:
time: 43.2 us; the launch traced here: 42.9 us
  Pallas kernels  34.1 us (79%)
  local copies, waits for them, and re-layouts  8.14 us (19%)
  between operations  0.66 us (2%)
    pallas_call x1, Pallas kernels, by_kernel(): pl.pallas_call(functools.partial(kernel, nz, nl), out_shape=(jax.ShapeDty...  34.1 us
    unnamed x20, local copies, waits for them, and re-layouts  8.14 us

profile of v1, /device:TPU:0, one launch (start us, length us, event | category | flops | bytes accessed | tf_op | source)
XLA Modules:
  0.0 42.9 jit_solution(13262131776472047401)
XLA Ops:
  0.6 0.0 copy-start
  0.6 1.0 %copy-done = bf16[1,16,128,128]{3,2,1,0:T(8,128)(2,1)S(1)} copy-done((bf16[1,16,128,128]{3,2,1,0:T(8,128)(2,1)S(1)}, bf16[1,16,128,128]{3,2,1,0:T(8,128)(2,1)}, u32[]{:S(2)}) %copy-start) | copy-done | bytes 524312
  1.7 0.0 copy-start.1
  1.7 0.8 %copy-done.1 = bf16[2,1,128,128]{3,2,1,0:T(8,128)(2,1)S(1)} copy-done((bf16[2,1,128,128]{3,2,1,0:T(8,128)(2,1)S(1)}, bf16[2,1,128,128]{3,2,1,0:T(8,128)(2,1)}, u32[]{:S(2)}) %copy-start.1) | copy-done | bytes 65560
  2.5 0.0 copy-start.2
  2.5 0.8 %copy-done.2 = bf16[2,1,128,128]{3,2,1,0:T(8,128)(2,1)S(1)} copy-done((bf16[2,1,128,128]{3,2,1,0:T(8,128)(2,1)S(1)}, bf16[2,1,128,128]{3,2,1,0:T(8,128)(2,1)}, u32[]{:S(2)}) %copy-start.2) | copy-done | bytes 65560
  3.4 0.0 copy-start.3
  3.4 0.7 %copy-done.3 = s32[16]{0:T(128)S(1)} copy-done((s32[16]{0:T(128)S(1)}, s32[16]{0:T(128)}, u32[]{:S(2)}) %copy-start.3) | copy-done | bytes 88
  4.0 0.0 copy-start.4
  4.0 0.7 %copy-done.4 = s32[16]{0:T(128)S(1)} copy-done((s32[16]{0:T(128)S(1)}, s32[16]{0:T(128)}, u32[]{:S(2)}) %copy-start.4) | copy-done | bytes 88
  4.7 0.0 copy-start.5
  4.7 0.7 %copy-done.5 = s32[16]{0:T(128)S(1)} copy-done((s32[16]{0:T(128)S(1)}, s32[16]{0:T(128)}, u32[]{:S(2)}) %copy-start.5) | copy-done | bytes 88
  5.3 0.0 copy-start.6
  5.3 0.7 %copy-done.6 = s32[16]{0:T(128)S(1)} copy-done((s32[16]{0:T(128)S(1)}, s32[16]{0:T(128)}, u32[]{:S(2)}) %copy-start.6) | copy-done | bytes 88
  6.0 0.0 copy-start.7
  6.0 0.7 %copy-done.7 = s32[16]{0:T(128)S(1)} copy-done((s32[16]{0:T(128)S(1)}, s32[16]{0:T(128)}, u32[]{:S(2)}) %copy-start.7) | copy-done | bytes 88
  6.6 0.0 copy-start.8
  6.6 0.7 %copy-done.8 = s32[16]{0:T(128)S(1)} copy-done((s32[16]{0:T(128)S(1)}, s32[16]{0:T(128)}, u32[]{:S(2)}) %copy-start.8) | copy-done | bytes 88
  7.3 34.1 %shard_map.104 = (bf16[1,16,128,128]{3,2,1,0:T(8,128)(2,1)S(1)}, bf16[1,8,128,128]{3,2,1,0:T(8,128)(2,1)S(1)}) custom-call(bf16[1,16,128,128]{3,2,1,0:T(8,128)(2,1)S(1)} %copy-done, bf16[2,1,128,128]{3,2,1,0:T(8,128)(2,1)S(1)} %copy-done.1, bf16[2,1,128,128]{3,2,1,0:T(8,128)(2,1)S(1)} %copy-done.2, s32[16]{0:T(128)S(1)} %copy-done.3, s32[16]{0:T(128)S(1)} %copy-done.4, ...), custom_call_target="tpu_custom_call" | custom-call | flops 805306368 | bytes 4194304 | tf_op jit(solution)/shard_map/pallas_call | solution.py:324
  41.4 0.8 %copy.13 = bf16[1,16,128,128]{3,2,1,0:T(8,128)(2,1)} copy(bf16[1,16,128,128]{3,2,1,0:T(8,128)(2,1)S(1)} %get-tuple-element.4) | data formatting | bytes 1048576
  42.2 0.7 %copy.14 = bf16[1,8,128,128]{3,2,1,0:T(8,128)(2,1)} copy(bf16[1,8,128,128]{3,2,1,0:T(8,128)(2,1)S(1)} %get-tuple-element.5) | data formatting | bytes 524288
Async XLA Ops:
  0.6 1.0 %copy-start = (bf16[1,16,128,128]{3,2,1,0:T(8,128)(2,1)S(1)}, bf16[1,16,128,128]{3,2,1,0:T(8,128)(2,1)}, u32[]{:S(2)}) copy-start(bf16[1,16,128,128]{3,2,1,0:T(8,128)(2,1)} %psi_ref.1) | copy-start | bytes 1572868
  1.7 0.8 %copy-start.1 = (bf16[2,1,128,128]{3,2,1,0:T(8,128)(2,1)S(1)}, bf16[2,1,128,128]{3,2,1,0:T(8,128)(2,1)}, u32[]{:S(2)}) copy-start(bf16[2,1,128,128]{3,2,1,0:T(8,128)(2,1)} %left_ref.1) | copy-start | bytes 196612
  2.5 0.8 %copy-start.2 = (bf16[2,1,128,128]{3,2,1,0:T(8,128)(2,1)S(1)}, bf16[2,1,128,128]{3,2,1,0:T(8,128)(2,1)}, u32[]{:S(2)}) copy-start(bf16[2,1,128,128]{3,2,1,0:T(8,128)(2,1)} %right_ref.1) | copy-start | bytes 196612
  3.4 0.7 %copy-start.3 = (s32[16]{0:T(128)S(1)}, s32[16]{0:T(128)}, u32[]{:S(2)}) copy-start(s32[16]{0:T(128)} %left_order.1) | copy-start | bytes 196
  4.0 0.7 %copy-start.4 = (s32[16]{0:T(128)S(1)}, s32[16]{0:T(128)}, u32[]{:S(2)}) copy-start(s32[16]{0:T(128)} %right_order.1) | copy-start | bytes 196
  4.7 0.7 %copy-start.5 = (s32[16]{0:T(128)S(1)}, s32[16]{0:T(128)}, u32[]{:S(2)}) copy-start(s32[16]{0:T(128)} %left_qn.1) | copy-start | bytes 196
  5.3 0.7 %copy-start.6 = (s32[16]{0:T(128)S(1)}, s32[16]{0:T(128)}, u32[]{:S(2)}) copy-start(s32[16]{0:T(128)} %right_qn.1) | copy-start | bytes 196
  6.0 0.7 %copy-start.7 = (s32[16]{0:T(128)S(1)}, s32[16]{0:T(128)}, u32[]{:S(2)}) copy-start(s32[16]{0:T(128)} %left_dims.1) | copy-start | bytes 196
  6.6 0.7 %copy-start.8 = (s32[16]{0:T(128)S(1)}, s32[16]{0:T(128)}, u32[]{:S(2)}) copy-start(s32[16]{0:T(128)} %right_dims.1) | copy-start | bytes 196

commit v2 on v1

--- a/solution.py
+++ b/solution.py
@@ -75,17 +75,25 @@
 def kernel(
     nz,
     nl,
-    psi_ref,
-    left_ref,
-    right_ref,
+    psi_hbm,
+    left_hbm,
+    right_hbm,
+    left_order_hbm,
+    right_order_hbm,
+    left_qn_hbm,
+    right_qn_hbm,
+    left_dims_hbm,
+    right_dims_hbm,
+    first_ref,
+    second_ref,
+    psi,
     left_order,
     right_order,
     left_qn,
     right_qn,
     left_dims,
     right_dims,
-    first_ref,
-    second_ref,
+    lsem,
     rbuf,
     lbuf,
     start,
@@ -115,8 +123,8 @@
     op = 1 - o
     me = l * nz + z
     slots = nl * nz
-    width = psi_ref.shape[-1]
-    kdev = left_ref.shape[0]
+    width = psi.shape[-1]
+    kdev = lbuf.shape[1]
     to_y = {"ops": op}
     to_x = {"lsec": xp}
     to_c = {"lsec": cp}
@@ -137,8 +145,24 @@
     def arrive(ref, sem):
         pltpu.make_async_copy(ref, ref, sem).wait()
 
-    rbuf[o, me] = right_ref[:, 0]
-    lbuf[o] = left_ref[:, 0]
+    loads = [
+        pltpu.make_async_copy(src, dst, lsem.at[i])
+        for i, (src, dst) in enumerate(
+            (
+                (right_hbm.at[:, 0], rbuf.at[o, me]),
+                (left_hbm.at[:, 0], lbuf.at[o]),
+                (left_order_hbm, left_order),
+                (right_order_hbm, right_order),
+                (left_qn_hbm, left_qn),
+                (right_qn_hbm, right_qn),
+                (left_dims_hbm, left_dims),
+                (right_dims_hbm, right_dims),
+                (psi_hbm.at[0], psi),
+            )
+        )
+    ]
+    for load in loads:
+        load.start()
 
     barrier = pltpu.get_barrier_semaphore()
     for s in range(nz):
@@ -156,7 +180,7 @@
     def slot_of(lane, s):
         return lane * nz + (z + s) % nz
 
-    send(lbuf.at[o], lbuf.at[o], lsend, lrecv, to_y)
+    loads[0].wait()
 
     def stage_one(s):
         if s:
@@ -195,6 +219,10 @@
         piece = rbuf.at[o, me]
         send(piece, piece, zsend.at[s], zrecv.at[s], {"rsec": (z + nz - s) % nz})
     stage_one(0)
+    loads[1].wait()
+    send(lbuf.at[o], lbuf.at[o], lsend, lrecv, to_y)
+    for load in loads[2:]:
+        load.wait()
 
     sector = left_order[me]
     my_qn = left_qn[sector]
@@ -206,32 +234,31 @@
         used = jnp.where(jnp.abs(my_qn - right_qn[b]) <= SPREAD, right_dims[b], 0)
         return jnp.where(rows_used & (cols < used), value, 0.0).astype(jnp.bfloat16)
 
-    def left_terms(half, pair):
-        both = jnp.dot(
-            lbuf[half].reshape(kdev * width, width), start[pair], preferred_element_type=jnp.float32
-        ).astype(jnp.bfloat16)
-        both = both.reshape(kdev, width, 2 * width)
-        terms[2 * pair, half] = both[:, :, :width]
-        terms[2 * pair + 1, half] = both[:, :, width:]
-
-    def own_terms(pair, carry):
+    def start_pair(pair, carry):
         blocks = []
         for j in (2 * pair, 2 * pair + 1):
             b = right_order[j]
-            blocks.append(masked(psi_ref[0, b].astype(jnp.float32), b))
+            blocks.append(masked(psi[b].astype(jnp.float32), b))
         start[pair] = jnp.concatenate(blocks, axis=1)
-        left_terms(o, pair)
         return carry
 
-    def other_terms(pair, carry):
-        left_terms(op, pair)
+    def terms_pair(pair, carry):
+        for h in range(2):
+            both = jnp.dot(
+                lbuf[h].reshape(kdev * width, width),
+                start[pair],
+                preferred_element_type=jnp.float32,
+            )
+            both = both.astype(jnp.bfloat16).reshape(kdev, width, 2 * width)
+            terms[2 * pair, h] = both[:, :, :width]
+            terms[2 * pair + 1, h] = both[:, :, width:]
         return carry
 
-    lax.fori_loop(0, slots // 2, own_terms, 0)
+    lax.fori_loop(0, slots // 2, start_pair, 0, unroll=2)
+    arrive(lbuf.at[op], lrecv)
     stage_one(1)
+    lax.fori_loop(0, slots // 2, terms_pair, 0, unroll=2)
     stage_two(0)
-    arrive(lbuf.at[op], lrecv)
-    lax.fori_loop(0, slots // 2, other_terms, 0)
 
     def lanes(ref, j):
         return jnp.concatenate([ref[j, h, k] for h in range(2) for k in range(kdev)], axis=1)
@@ -278,22 +305,32 @@
 
     count = second_ref.shape[1]
 
-    def second_block(i, carry):
-        b = o * count + i
-        j = slot_holding(right_order, b)
-        state = sigma[j]
-        value = None
-        for h in range(2):
-            for k in range(kdev):
-                inner = lax.dot_general(
-                    state, rbuf[h, j, k], NT, preferred_element_type=jnp.float32
+    left_wide = jnp.concatenate([lbuf[h, k] for h in range(2) for k in range(kdev)], axis=1)
+
+    def second_pair(i, carry):
+        inner = []
+        for n in range(2):
+            j = slot_holding(right_order, o * count + 2 * i + n)
+            halves = []
+            for h in range(2):
+                part = lax.dot_general(
+                    sigma[j],
+                    rbuf[h, j].reshape(kdev * width, width),
+                    NT,
+                    preferred_element_type=jnp.float32,
                 ).astype(jnp.bfloat16)
-                outer = jnp.dot(lbuf[h, k], inner, preferred_element_type=jnp.float32)
-                value = outer if value is None else value + outer
-        second_ref[0, i] = masked(value, b)
+                halves += [part[:, k * width : (k + 1) * width] for k in range(kdev)]
+            inner.append(jnp.concatenate(halves, axis=0))
+        both = jnp.dot(
+            left_wide, jnp.concatenate(inner, axis=1), preferred_element_type=jnp.float32
+        )
+        for n in range(2):
+            second_ref[0, 2 * i + n] = masked(
+                both[:, n * width : (n + 1) * width], o * count + 2 * i + n
+            )
         return carry
 
-    lax.fori_loop(0, count, second_block, 0, unroll=2)
+    lax.fori_loop(0, count // 2, second_pair, 0)
 
     for s in range(nz):
         for t in range(nl):
@@ -319,7 +356,7 @@
     dma = pltpu.SemaphoreType.DMA
     bf16 = jnp.bfloat16
     vmem = pl.BlockSpec(memory_space=pltpu.VMEM)
-    smem = pl.BlockSpec(memory_space=pltpu.SMEM)
+    hbm = pl.BlockSpec(memory_space=pltpu.HBM)
     flops = 2 * width**3 * 2 * kdev * slots * 3
     return pl.pallas_call(
         functools.partial(kernel, nz, nl),
@@ -327,9 +364,12 @@
             jax.ShapeDtypeStruct((1, slots) + block, bf16),
             jax.ShapeDtypeStruct((1, slots // 2) + block, bf16),
         ),
-        in_specs=[vmem] * 3 + [smem] * 6,
+        in_specs=[hbm] * 9,
         out_specs=(vmem, vmem),
         scratch_shapes=[
+            pltpu.VMEM((slots,) + block, bf16),
+            *[pltpu.SMEM(table.shape, jnp.int32) for table in tables],
+            dma((9,)),
             pltpu.VMEM((2, slots, kdev) + block, bf16),
             pltpu.VMEM((2, kdev) + block, bf16),
             pltpu.VMEM((slots // 2, width, 2 * width), bf16),
@@ -352,7 +392,7 @@
             dma((nz, nl)),
         ],
         compiler_params=pltpu.CompilerParams(
-            collective_id=0, has_side_effects=True, vmem_limit_bytes=40 * 2**20
+            collective_id=0, has_side_effects=True, vmem_limit_bytes=56 * 2**20
         ),
         cost_estimate=pl.CostEstimate(flops=flops, bytes_accessed=4 * 2**20, transcendentals=0),
     )(psi, left_ops, right_ops, *tables)
@@ -363,7 +403,7 @@
 
     def on_device(psi, left_ops, right_ops, *tables):
         gathered = no * nl * nz * left_ops.size * left_ops.dtype.itemsize
-        if no == 2 and nl == 4 and left_ops.shape[0] > 1 and 3 * gathered <= VMEM_BUDGET:
+        if no == 2 and nl == 4 and nz > 1 and left_ops.shape[0] > 1 and 3 * gathered <= VMEM_BUDGET:
             return by_kernel(nz, nl, psi, left_ops, right_ops, *tables)
         return by_collectives(psi, left_ops, right_ops, *tables)
 

time: 43.2 us -> 38.1 us (0.88)
  local copies, waits for them, and re-layouts: 8.14 us -> 2.63 us
  Pallas kernels: 34.1 us -> 34.7 us
    unnamed x20 -> x4, local copies, waits for them, and re-layouts: 8.14 us -> 2.63 us
    pallas_call x1, Pallas kernels: 34.1 us -> 34.7 us  [by_kernel(): pl.pallas_call(functools.partial(kernel, nz, nl), out_shape=(jax.ShapeDty...]
where the time goes in v2:
time: 38.1 us; the launch traced here: 38 us
  Pallas kernels  34.7 us (91%)
  local copies, waits for them, and re-layouts  2.63 us (7%)
  between operations  0.65 us (2%)
    pallas_call x1, Pallas kernels, by_kernel(): pl.pallas_call(functools.partial(kernel, nz, nl), out_shape=(jax.ShapeDty...  34.7 us
    unnamed x4, local copies, waits for them, and re-layouts  2.63 us

profile of v2, /device:TPU:0, one launch (start us, length us, event | category | flops | bytes accessed | tf_op | source)
XLA Modules:
  0.0 38.0 jit_solution(13094136631700074853)
XLA Ops:
  0.6 34.7 %shard_map.104 = (bf16[1,16,128,128]{3,2,1,0:T(8,128)(2,1)}, bf16[1,8,128,128]{3,2,1,0:T(8,128)(2,1)}) custom-call(bf16[1,16,128,128]{3,2,1,0:T(8,128)(2,1)} %psi_hbm.1, bf16[2,1,128,128]{3,2,1,0:T(8,128)(2,1)} %left_hbm.1, bf16[2,1,128,128]{3,2,1,0:T(8,128)(2,1)} %right_hbm.1, s32[16]{0:T(128)} %left_order_hbm.1, s32[16]{0:T(128)} %right_order_hbm.1, ...), custom_call_target="tpu_custom_call" | custom-call | flops 805306368 | bytes 4194304 | tf_op jit(solution)/shard_map/pallas_call | solution.py:361
  35.3 0.0 copy-start
  35.3 1.9 %copy.13 = bf16[1,16,128,128]{3,2,1,0:T(8,128)(2,1)} copy(bf16[1,16,128,128]{3,2,1,0:T(8,128)(2,1)} %get-tuple-element.4) | data formatting | bytes 1048576
  37.2 0.0 copy-done
  37.3 0.7 %copy.14 = bf16[1,8,128,128]{3,2,1,0:T(8,128)(2,1)} copy(bf16[1,8,128,128]{3,2,1,0:T(8,128)(2,1)S(1)} %copy-done) | data formatting | bytes 524288
Async XLA Ops:
  35.3 1.9 %copy-start = (bf16[1,8,128,128]{3,2,1,0:T(8,128)(2,1)S(1)}, bf16[1,8,128,128]{3,2,1,0:T(8,128)(2,1)}, u32[]{:S(2)}) copy-start(bf16[1,8,128,128]{3,2,1,0:T(8,128)(2,1)} %get-tuple-element.5) | copy-start | bytes 786436

commit v3 on v2

--- a/solution.py
+++ b/solution.py
@@ -114,6 +114,12 @@
     crecv,
     ssend,
     srecv,
+    fsend,
+    frecv,
+    first,
+    second,
+    inverse_left,
+    osem,
 ):
     l = lax.axis_index("lsec")
     z = lax.axis_index("rsec")
@@ -149,7 +155,7 @@
         pltpu.make_async_copy(src, dst, lsem.at[i])
         for i, (src, dst) in enumerate(
             (
-                (right_hbm.at[:, 0], rbuf.at[o, me]),
+                (right_hbm.at[:, 0], rbuf.at[me, o]),
                 (left_hbm.at[:, 0], lbuf.at[o]),
                 (left_order_hbm, left_order),
                 (right_order_hbm, right_order),
@@ -183,40 +189,34 @@
     loads[0].wait()
 
     def stage_one(s):
+        piece = rbuf.at[slot_of(l, s), o]
         if s:
-            arrive(rbuf.at[o, slot_of(l, s)], zrecv.at[s])
-        piece = rbuf.at[o, slot_of(l, s)]
+            arrive(piece, zrecv.at[s])
         send(piece, piece, ysend.at[s], yrecv.at[s], to_y)
         send(piece, piece, xsend.at[s], xrecv.at[s], to_x)
-        send(piece, piece, csend.at[0, s], crecv.at[0, s], to_c)
 
     def stage_two(s):
-        from_x = rbuf.at[o, slot_of(xp, s)]
-        arrive(from_x, xrecv.at[s])
-        half = rbuf.at[o, slot_of(xp, s), 0]
+        mine, theirs = slot_of(l, s), slot_of(xp, s)
+        arrive(rbuf.at[theirs, o], xrecv.at[s])
+        half = rbuf.at[theirs, o, 0]
         send(half, half, dsend.at[0, s], drecv.at[0, s], to_y)
-        send(from_x, from_x, csend.at[1, s], crecv.at[1, s], to_c)
-        from_y = rbuf.at[op, slot_of(l, s)]
-        arrive(from_y, yrecv.at[s])
-        rest = rbuf.at[op, slot_of(l, s), pl.ds(1, kdev - 1)]
+        arrive(rbuf.at[mine, op], yrecv.at[s])
+        rest = rbuf.at[mine, op, pl.ds(1, kdev - 1)]
         send(rest, rest, dsend.at[1, s], drecv.at[1, s], to_x)
-        send(from_y, from_y, csend.at[2, s], crecv.at[2, s], to_c)
+        send(rbuf.at[mine], rbuf.at[mine], csend.at[0, s], crecv.at[0, s], to_c)
 
     def stage_three(s):
-        piece = rbuf.at[op, slot_of(xp, s)]
-        arrive(rbuf.at[op, slot_of(xp, s), 0], drecv.at[0, s])
-        arrive(rbuf.at[op, slot_of(xp, s), pl.ds(1, kdev - 1)], drecv.at[1, s])
-        send(piece, piece, csend.at[3, s], crecv.at[3, s], to_c)
+        theirs = slot_of(xp, s)
+        arrive(rbuf.at[theirs, op, 0], drecv.at[0, s])
+        arrive(rbuf.at[theirs, op, pl.ds(1, kdev - 1)], drecv.at[1, s])
+        send(rbuf.at[theirs], rbuf.at[theirs], csend.at[1, s], crecv.at[1, s], to_c)
 
     def stage_four(s):
-        cx = (cp + 2) % nl
-        arrive(rbuf.at[o, slot_of(cp, s)], crecv.at[0, s])
-        arrive(rbuf.at[o, slot_of(cx, s)], crecv.at[1, s])
-        arrive(rbuf.at[op, slot_of(cp, s)], crecv.at[2, s])
-        arrive(rbuf.at[op, slot_of(cx, s)], crecv.at[3, s])
+        arrive(rbuf.at[slot_of(cp, s)], crecv.at[0, s])
+        arrive(rbuf.at[slot_of((cp + 2) % nl, s)], crecv.at[1, s])
 
     for s in range(1, nz):
-        piece = rbuf.at[o, me]
+        piece = rbuf.at[me, o]
         send(piece, piece, zsend.at[s], zrecv.at[s], {"rsec": (z + nz - s) % nz})
     stage_one(0)
     loads[1].wait()
@@ -254,38 +254,56 @@
             terms[2 * pair + 1, h] = both[:, :, width:]
         return carry
 
-    lax.fori_loop(0, slots // 2, start_pair, 0, unroll=2)
-    arrive(lbuf.at[op], lrecv)
-    stage_one(1)
-    lax.fori_loop(0, slots // 2, terms_pair, 0, unroll=2)
-    stage_two(0)
-
     def lanes(ref, j):
         return jnp.concatenate([ref[j, h, k] for h in range(2) for k in range(kdev)], axis=1)
 
-    def right_lanes(j):
-        return jnp.concatenate([rbuf[h, j, k] for h in range(2) for k in range(kdev)], axis=1)
-
-    def first_blocks(s):
-        for t in range(nl):
-            j = slot_of((l + t) % nl, s)
-            value = lax.dot_general(
-                lanes(terms, j), right_lanes(j), NT, preferred_element_type=jnp.float32
+    def first_block(j):
+        value = lax.dot_general(
+            lanes(terms, j), lanes(rbuf, j), NT, preferred_element_type=jnp.float32
+        )
+        sigma[j] = masked(value, right_order[j])
+
+    def direct(plane, s):
+        if s == 0:
+            return [1 + 2 * plane, 2]
+        return [2 * u + (plane + s) % 2 for u in range(nl // 2)]
+
+    def others(plane, s):
+        if s == 0:
+            return [0, 3 - 2 * plane]
+        return [2 * u + (plane + s + 1) % 2 for u in range(nl // 2)]
+
+    def relayed(s):
+        return range(1 if s == 0 else nl // 2)
+
+    def source_of(s, t):
+        return ((l + nl - t) % nl) * nz + (z + nz - s) % nz
+
+    def first_direct(s):
+        targets = [(l + t) % nl for t in direct(o, s)]
+        for there in targets:
+            first_block(slot_of(there, s))
+        for u, there in enumerate(targets):
+            send(
+                sigma.at[slot_of(there, s)],
+                landed.at[me],
+                ssend.at[s, u],
+                srecv.at[s, u],
+                {"lsec": there, "rsec": (z + s) % nz},
             )
-            sigma[j] = masked(value, right_order[j])
-        for t in range(nl):
-            j = slot_of((l + t) % nl, s)
-            if s or t:
-                send(
-                    sigma.at[j],
-                    landed.at[me],
-                    ssend.at[s, t],
-                    srecv.at[s, t],
-                    {"lsec": (l + t) % nl, "rsec": (z + s) % nz},
-                )
-            else:
-                landed[me] = sigma[j]
-
+
+    def relay(s):
+        for u in relayed(s):
+            block = landed.at[source_of(s, direct(o, s)[u])]
+            arrive(block, srecv.at[s, u])
+            send(block, block, fsend.at[s, u], frecv.at[s, u], to_y)
+
+    lax.fori_loop(0, slots // 2, start_pair, 0, unroll=2)
+    stage_one(1)
+    stage_two(0)
+    arrive(lbuf.at[op], lrecv)
+    quarter = slots // 4
+    lax.fori_loop(0, quarter, terms_pair, 0, unroll=2)
     for step in range(2, nz + 3):
         if step < nz:
             stage_one(step)
@@ -293,9 +311,19 @@
             stage_two(step - 1)
         if 0 <= step - 2 < nz:
             stage_three(step - 2)
+        if step == 2:
+            lax.fori_loop(quarter, 2 * quarter, terms_pair, 0, unroll=2)
         if 0 <= step - 3 < nz:
             stage_four(step - 3)
-            first_blocks(step - 3)
+            first_direct(step - 3)
+        if 0 <= step - 5 < nz - 2:
+            relay(step - 5)
+
+    for s in range(nz):
+        for t in others(o, s):
+            first_block(slot_of((l + t) % nl, s))
+    landed[me] = sigma[me]
+    relay(nz - 2)
 
     def slot_holding(order, wanted):
         found = jnp.int32(0)
@@ -304,7 +332,6 @@
         return found
 
     count = second_ref.shape[1]
-
     left_wide = jnp.concatenate([lbuf[h, k] for h in range(2) for k in range(kdev)], axis=1)
 
     def second_pair(i, carry):
@@ -315,7 +342,7 @@
             for h in range(2):
                 part = lax.dot_general(
                     sigma[j],
-                    rbuf[h, j].reshape(kdev * width, width),
+                    rbuf[j, h].reshape(kdev * width, width),
                     NT,
                     preferred_element_type=jnp.float32,
                 ).astype(jnp.bfloat16)
@@ -325,27 +352,53 @@
             left_wide, jnp.concatenate(inner, axis=1), preferred_element_type=jnp.float32
         )
         for n in range(2):
-            second_ref[0, 2 * i + n] = masked(
+            second[2 * i + n] = masked(
                 both[:, n * width : (n + 1) * width], o * count + 2 * i + n
             )
         return carry
 
-    lax.fori_loop(0, count // 2, second_pair, 0)
-
+    lax.fori_loop(0, count // 4, second_pair, 0)
+    relay(nz - 1)
+    lax.fori_loop(count // 4, count // 2, second_pair, 0)
+    out_second = pltpu.make_async_copy(second, second_ref.at[0], osem.at[0])
+    out_second.start()
+
+    def find(a, carry):
+        inverse_left[a] = slot_holding(left_order, a)
+        return carry
+
+    lax.fori_loop(0, slots, find, 0)
+
+    arrive(landed.at[source_of(0, 2)], srecv.at[0, 1])
     for s in range(nz):
-        for t in range(nl):
-            if s or t:
-                source = ((l + nl - t) % nl) * nz + (z + nz - s) % nz
-                arrive(landed.at[source], srecv.at[s, t])
+        for u in relayed(s):
+            arrive(landed.at[source_of(s, direct(op, s)[u])], frecv.at[s, u])
 
     def place(a, carry):
-        first_ref[0, a] = landed[slot_holding(left_order, a)]
+        first[a] = landed[inverse_left[a]]
         return carry
 
-    lax.fori_loop(0, slots, place, 0)
-
+    lax.fori_loop(0, slots, place, 0, unroll=4)
+    out_first = pltpu.make_async_copy(first, first_ref.at[0], osem.at[1])
+    out_first.start()
     for copy in sent:
         copy.wait_send()
+    out_second.wait()
+    out_first.wait()
+
+
+def hand_over(parts, *refs):
+    count = len(refs) // 3
+    copies = []
+    for src, dst, sem in zip(refs[:count], refs[count : 2 * count], refs[2 * count :]):
+        size = src.shape[1] // parts
+        for i in range(parts):
+            rows = pl.ds(i * size, size)
+            copies.append(pltpu.make_async_copy(src.at[:, rows], dst.at[:, rows], sem.at[i]))
+    for copy in copies:
+        copy.start()
+    for copy in copies:
+        copy.wait()
 
 
 def by_kernel(nz, nl, psi, left_ops, right_ops, *tables):
@@ -355,22 +408,22 @@
     block = (width, width)
     dma = pltpu.SemaphoreType.DMA
     bf16 = jnp.bfloat16
-    vmem = pl.BlockSpec(memory_space=pltpu.VMEM)
     hbm = pl.BlockSpec(memory_space=pltpu.HBM)
     flops = 2 * width**3 * 2 * kdev * slots * 3
-    return pl.pallas_call(
+    shapes = (
+        jax.ShapeDtypeStruct((1, slots) + block, bf16),
+        jax.ShapeDtypeStruct((1, slots // 2) + block, bf16),
+    )
+    results = pl.pallas_call(
         functools.partial(kernel, nz, nl),
-        out_shape=(
-            jax.ShapeDtypeStruct((1, slots) + block, bf16),
-            jax.ShapeDtypeStruct((1, slots // 2) + block, bf16),
-        ),
+        out_shape=shapes,
         in_specs=[hbm] * 9,
-        out_specs=(vmem, vmem),
+        out_specs=(hbm, hbm),
         scratch_shapes=[
             pltpu.VMEM((slots,) + block, bf16),
             *[pltpu.SMEM(table.shape, jnp.int32) for table in tables],
             dma((9,)),
-            pltpu.VMEM((2, slots, kdev) + block, bf16),
+            pltpu.VMEM((slots, 2, kdev) + block, bf16),
             pltpu.VMEM((2, kdev) + block, bf16),
             pltpu.VMEM((slots // 2, width, 2 * width), bf16),
             pltpu.VMEM((slots, 2, kdev) + block, bf16),
@@ -386,16 +439,31 @@
             dma((nz,)),
             dma((2, nz)),
             dma((2, nz)),
-            dma((4, nz)),
-            dma((4, nz)),
-            dma((nz, nl)),
-            dma((nz, nl)),
+            dma((2, nz)),
+            dma((2, nz)),
+            dma((nz, nl // 2)),
+            dma((nz, nl // 2)),
+            dma((nz, nl // 2)),
+            dma((nz, nl // 2)),
+            pltpu.VMEM((slots,) + block, bf16),
+            pltpu.VMEM((slots // 2,) + block, bf16),
+            pltpu.SMEM((slots,), jnp.int32),
+            dma((2,)),
         ],
         compiler_params=pltpu.CompilerParams(
             collective_id=0, has_side_effects=True, vmem_limit_bytes=56 * 2**20
         ),
         cost_estimate=pl.CostEstimate(flops=flops, bytes_accessed=4 * 2**20, transcendentals=0),
     )(psi, left_ops, right_ops, *tables)
+    parts = 4
+    return pl.pallas_call(
+        functools.partial(hand_over, parts),
+        out_shape=shapes,
+        in_specs=[hbm] * 2,
+        out_specs=(hbm, hbm),
+        scratch_shapes=[dma((parts,)), dma((parts,))],
+        compiler_params=pltpu.CompilerParams(vmem_limit_bytes=56 * 2**20),
+    )(*results)
 
 
 def solution(mesh):
@@ -403,7 +471,7 @@
 
     def on_device(psi, left_ops, right_ops, *tables):
         gathered = no * nl * nz * left_ops.size * left_ops.dtype.itemsize
-        if no == 2 and nl == 4 and nz > 1 and left_ops.shape[0] > 1 and 3 * gathered <= VMEM_BUDGET:
+        if no == 2 and nl == 4 and nz > 2 and left_ops.shape[0] > 1 and 3 * gathered <= VMEM_BUDGET:
             return by_kernel(nz, nl, psi, left_ops, right_ops, *tables)
         return by_collectives(psi, left_ops, right_ops, *tables)
 

time: 38.1 us -> 58.9 us (1.55)
  Pallas kernels: 34.7 us -> 58.1 us
  local copies, waits for them, and re-layouts: 2.63 us -> 0 us
    pallas_call x1 -> x2, Pallas kernels: 34.7 us -> 58.1 us  [the longest x1 33.1 us: by_kernel(): pl.pallas_call(functools.partial(kernel, nz, nl), out_shape=shapes, in_sp...]
    unnamed x4 -> x0, local copies, waits for them, and re-layouts: 2.63 us -> none
where the time goes in v3:
time: 58.9 us; the launch traced here: 58.7 us
  Pallas kernels  58.1 us (99%)
  between operations  0.64 us (1%)
    pallas_call x1, Pallas kernels, by_kernel(): pl.pallas_call(functools.partial(kernel, nz, nl), out_shape=shapes, in_sp...  33.1 us
    pallas_call x1, Pallas kernels, by_kernel(): pl.pallas_call(functools.partial(hand_over, parts), out_shape=shapes, in_...  25 us

profile of v3, /device:TPU:0, one launch (start us, length us, event | category | flops | bytes accessed | tf_op | source)
XLA Modules:
  0.0 58.7 jit_solution(8303510328385770097)
XLA Ops:
  0.6 33.1 %shard_map.104 = (bf16[1,16,128,128]{3,2,1,0:T(8,128)(2,1)}, bf16[1,8,128,128]{3,2,1,0:T(8,128)(2,1)}) custom-call(bf16[1,16,128,128]{3,2,1,0:T(8,128)(2,1)} %psi_hbm.1, bf16[2,1,128,128]{3,2,1,0:T(8,128)(2,1)} %left_hbm.1, bf16[2,1,128,128]{3,2,1,0:T(8,128)(2,1)} %right_hbm.1, s32[16]{0:T(128)} %left_order_hbm.1, s32[16]{0:T(128)} %right_order_hbm.1, ...), custom_call_target="tpu_custom_call" | custom-call | flops 805306368 | bytes 4194304 | tf_op jit(solution)/shard_map/pallas_call | solution.py:417
  33.7 25.0 %shard_map.105 = (bf16[1,16,128,128]{3,2,1,0:T(8,128)(2,1)}, bf16[1,8,128,128]{3,2,1,0:T(8,128)(2,1)}) custom-call(bf16[1,16,128,128]{3,2,1,0:T(8,128)(2,1)} %get-tuple-element.4.refs_0_, bf16[1,8,128,128]{3,2,1,0:T(8,128)(2,1)} %get-tuple-element.5.refs_1_), custom_call_target="tpu_custom_call" | custom-call | tf_op jit(solution)/shard_map/pallas_call | solution.py:459

commit v4 on v3

--- a/solution.py
+++ b/solution.py
@@ -198,17 +198,21 @@
     def stage_two(s):
         mine, theirs = slot_of(l, s), slot_of(xp, s)
         arrive(rbuf.at[theirs, o], xrecv.at[s])
-        half = rbuf.at[theirs, o, 0]
-        send(half, half, dsend.at[0, s], drecv.at[0, s], to_y)
+        cut = 0 if s == 1 else 1
+        if cut:
+            half = rbuf.at[theirs, o, 0]
+            send(half, half, dsend.at[0, s], drecv.at[0, s], to_y)
         arrive(rbuf.at[mine, op], yrecv.at[s])
-        rest = rbuf.at[mine, op, pl.ds(1, kdev - 1)]
+        rest = rbuf.at[mine, op, pl.ds(cut, kdev - cut)]
         send(rest, rest, dsend.at[1, s], drecv.at[1, s], to_x)
         send(rbuf.at[mine], rbuf.at[mine], csend.at[0, s], crecv.at[0, s], to_c)
 
     def stage_three(s):
         theirs = slot_of(xp, s)
-        arrive(rbuf.at[theirs, op, 0], drecv.at[0, s])
-        arrive(rbuf.at[theirs, op, pl.ds(1, kdev - 1)], drecv.at[1, s])
+        cut = 0 if s == 1 else 1
+        if cut:
+            arrive(rbuf.at[theirs, op, 0], drecv.at[0, s])
+        arrive(rbuf.at[theirs, op, pl.ds(cut, kdev - cut)], drecv.at[1, s])
         send(rbuf.at[theirs], rbuf.at[theirs], csend.at[1, s], crecv.at[1, s], to_c)
 
     def stage_four(s):
@@ -257,24 +261,19 @@
     def lanes(ref, j):
         return jnp.concatenate([ref[j, h, k] for h in range(2) for k in range(kdev)], axis=1)
 
-    def first_block(j):
+    def first_value(j, b):
         value = lax.dot_general(
             lanes(terms, j), lanes(rbuf, j), NT, preferred_element_type=jnp.float32
         )
-        sigma[j] = masked(value, right_order[j])
+        return masked(value, b)
+
+    def first_block(j):
+        sigma[j] = first_value(j, right_order[j])
 
     def direct(plane, s):
         if s == 0:
-            return [1 + 2 * plane, 2]
+            return list(range(1, nl))
         return [2 * u + (plane + s) % 2 for u in range(nl // 2)]
-
-    def others(plane, s):
-        if s == 0:
-            return [0, 3 - 2 * plane]
-        return [2 * u + (plane + s + 1) % 2 for u in range(nl // 2)]
-
-    def relayed(s):
-        return range(1 if s == 0 else nl // 2)
 
     def source_of(s, t):
         return ((l + nl - t) % nl) * nz + (z + nz - s) % nz
@@ -293,7 +292,7 @@
             )
 
     def relay(s):
-        for u in relayed(s):
+        for u in range(nl // 2):
             block = landed.at[source_of(s, direct(o, s)[u])]
             arrive(block, srecv.at[s, u])
             send(block, block, fsend.at[s, u], frecv.at[s, u], to_y)
@@ -302,6 +301,17 @@
     stage_one(1)
     stage_two(0)
     arrive(lbuf.at[op], lrecv)
+    def slot_holding(order, wanted):
+        found = jnp.int32(0)
+        for j in range(slots):
+            found = jnp.where(order[j] == wanted, j, found)
+        return found
+
+    def find(a, carry):
+        inverse_left[a] = slot_holding(left_order, a)
+        return carry
+
+    lax.fori_loop(0, slots, find, 0)
     quarter = slots // 4
     lax.fori_loop(0, quarter, terms_pair, 0, unroll=2)
     for step in range(2, nz + 3):
@@ -316,20 +326,12 @@
         if 0 <= step - 3 < nz:
             stage_four(step - 3)
             first_direct(step - 3)
-        if 0 <= step - 5 < nz - 2:
+        if 0 < step - 5 < nz - 2:
             relay(step - 5)
 
-    for s in range(nz):
-        for t in others(o, s):
-            first_block(slot_of((l + t) % nl, s))
+    first_block(me)
     landed[me] = sigma[me]
     relay(nz - 2)
-
-    def slot_holding(order, wanted):
-        found = jnp.int32(0)
-        for j in range(slots):
-            found = jnp.where(order[j] == wanted, j, found)
-        return found
 
     count = second_ref.shape[1]
     left_wide = jnp.concatenate([lbuf[h, k] for h in range(2) for k in range(kdev)], axis=1)
@@ -337,11 +339,13 @@
     def second_pair(i, carry):
         inner = []
         for n in range(2):
-            j = slot_holding(right_order, o * count + 2 * i + n)
+            b = o * count + 2 * i + n
+            j = slot_holding(right_order, b)
+            state = first_value(j, b)
             halves = []
             for h in range(2):
                 part = lax.dot_general(
-                    sigma[j],
+                    state,
                     rbuf[j, h].reshape(kdev * width, width),
                     NT,
                     preferred_element_type=jnp.float32,
@@ -363,15 +367,10 @@
     out_second = pltpu.make_async_copy(second, second_ref.at[0], osem.at[0])
     out_second.start()
 
-    def find(a, carry):
-        inverse_left[a] = slot_holding(left_order, a)
-        return carry
-
-    lax.fori_loop(0, slots, find, 0)
-
-    arrive(landed.at[source_of(0, 2)], srecv.at[0, 1])
-    for s in range(nz):
-        for u in relayed(s):
+    for u, t in enumerate(direct(o, 0)):
+        arrive(landed.at[source_of(0, t)], srecv.at[0, u])
+    for s in range(1, nz):
+        for u in range(nl // 2):
             arrive(landed.at[source_of(s, direct(op, s)[u])], frecv.at[s, u])
 
     def place(a, carry):
@@ -387,17 +386,22 @@
     out_first.wait()
 
 
-def hand_over(parts, *refs):
-    count = len(refs) // 3
-    copies = []
-    for src, dst, sem in zip(refs[:count], refs[count : 2 * count], refs[2 * count :]):
-        size = src.shape[1] // parts
+def hand_over(parts, first_in, second_in, first_out, second_out, first, second, sem):
+    ins, outs = [], []
+    for n, (src, mid, dst) in enumerate(
+        ((second_in, second, second_out), (first_in, first, first_out))
+    ):
+        size = mid.shape[0] // parts
         for i in range(parts):
             rows = pl.ds(i * size, size)
-            copies.append(pltpu.make_async_copy(src.at[:, rows], dst.at[:, rows], sem.at[i]))
-    for copy in copies:
+            ins.append(pltpu.make_async_copy(src.at[0, rows], mid.at[rows], sem.at[0, n, i]))
+            outs.append(pltpu.make_async_copy(mid.at[rows], dst.at[0, rows], sem.at[1, n, i]))
+    for copy in ins:
         copy.start()
-    for copy in copies:
+    for arrived, copy in zip(ins, outs):
+        arrived.wait()
+        copy.start()
+    for copy in outs:
         copy.wait()
 
 
@@ -441,8 +445,8 @@
             dma((2, nz)),
             dma((2, nz)),
             dma((2, nz)),
-            dma((nz, nl // 2)),
-            dma((nz, nl // 2)),
+            dma((nz, nl)),
+            dma((nz, nl)),
             dma((nz, nl // 2)),
             dma((nz, nl // 2)),
             pltpu.VMEM((slots,) + block, bf16),
@@ -461,7 +465,11 @@
         out_shape=shapes,
         in_specs=[hbm] * 2,
         out_specs=(hbm, hbm),
-        scratch_shapes=[dma((parts,)), dma((parts,))],
+        scratch_shapes=[
+            pltpu.VMEM((slots,) + block, bf16),
+            pltpu.VMEM((slots // 2,) + block, bf16),
+            dma((2, 2, parts)),
+        ],
         compiler_params=pltpu.CompilerParams(vmem_limit_bytes=56 * 2**20),
     )(*results)
 

time: 58.9 us -> 36.3 us (0.62)
  Pallas kernels: 58.1 us -> 35.5 us
    pallas_call x1, Pallas kernels: 25 us -> 2.01 us  [by_kernel(): pl.pallas_call(functools.partial(hand_over, parts), out_shape=shapes, in_...]
where the time goes in v4:
time: 36.3 us; the launch traced here: 36.2 us
  Pallas kernels  35.5 us (98%)
  between operations  0.64 us (2%)
    pallas_call x1, Pallas kernels, by_kernel(): pl.pallas_call(functools.partial(kernel, nz, nl), out_shape=shapes, in_sp...  33.5 us
    pallas_call x1, Pallas kernels, by_kernel(): pl.pallas_call(functools.partial(hand_over, parts), out_shape=shapes, in_...  2.01 us

profile of v4, /device:TPU:0, one launch (start us, length us, event | category | flops | bytes accessed | tf_op | source)
XLA Modules:
  0.0 36.2 jit_solution(13753208829197481445)
XLA Ops:
  0.6 33.5 %shard_map.104 = (bf16[1,16,128,128]{3,2,1,0:T(8,128)(2,1)}, bf16[1,8,128,128]{3,2,1,0:T(8,128)(2,1)}) custom-call(bf16[1,16,128,128]{3,2,1,0:T(8,128)(2,1)} %psi_hbm.1, bf16[2,1,128,128]{3,2,1,0:T(8,128)(2,1)} %left_hbm.1, bf16[2,1,128,128]{3,2,1,0:T(8,128)(2,1)} %right_hbm.1, s32[16]{0:T(128)} %left_order_hbm.1, s32[16]{0:T(128)} %right_order_hbm.1, ...), custom_call_target="tpu_custom_call" | custom-call | flops 805306368 | bytes 4194304 | tf_op jit(solution)/shard_map/pallas_call | solution.py:421
  34.2 2.0 %shard_map.105 = (bf16[1,16,128,128]{3,2,1,0:T(8,128)(2,1)}, bf16[1,8,128,128]{3,2,1,0:T(8,128)(2,1)}) custom-call(bf16[1,16,128,128]{3,2,1,0:T(8,128)(2,1)} %get-tuple-element.4.first_in, bf16[1,8,128,128]{3,2,1,0:T(8,128)(2,1)} %get-tuple-element.5.second_in), custom_call_target="tpu_custom_call" | custom-call | tf_op jit(solution)/shard_map/pallas_call | solution.py:463

commit v5 on v4

--- a/solution.py
+++ b/solution.py
@@ -10,7 +10,6 @@
 SPREAD = 1
 VMEM_BUDGET = 24 * 2**20
 MESH = pl.DeviceIdType.MESH
-NT = (((1,), (1,)), ((), ()))
 
 
 def relayout(blocks):
@@ -93,6 +92,7 @@
     right_qn,
     left_dims,
     right_dims,
+    right_own,
     lsem,
     rbuf,
     lbuf,
@@ -155,7 +155,7 @@
         pltpu.make_async_copy(src, dst, lsem.at[i])
         for i, (src, dst) in enumerate(
             (
-                (right_hbm.at[:, 0], rbuf.at[me, o]),
+                (right_hbm.at[:, 0], right_own),
                 (left_hbm.at[:, 0], lbuf.at[o]),
                 (left_order_hbm, left_order),
                 (right_order_hbm, right_order),
@@ -181,12 +181,13 @@
                     device_id_type=MESH,
                 )
     pl.semaphore_signal(barrier, inc=1, device_id=to_y, device_id_type=MESH)
+    loads[0].wait()
+    for k in range(kdev):
+        rbuf[me, o, k] = right_own[k].astype(jnp.float32).T.astype(jnp.bfloat16)
     pl.semaphore_wait(barrier, slots)
 
     def slot_of(lane, s):
         return lane * nz + (z + s) % nz
-
-    loads[0].wait()
 
     def stage_one(s):
         piece = rbuf.at[slot_of(l, s), o]
@@ -262,8 +263,10 @@
         return jnp.concatenate([ref[j, h, k] for h in range(2) for k in range(kdev)], axis=1)
 
     def first_value(j, b):
-        value = lax.dot_general(
-            lanes(terms, j), lanes(rbuf, j), NT, preferred_element_type=jnp.float32
+        value = jnp.dot(
+            lanes(terms, j),
+            rbuf[j].reshape(2 * kdev * width, width),
+            preferred_element_type=jnp.float32,
         )
         return masked(value, b)
 
@@ -342,15 +345,9 @@
             b = o * count + 2 * i + n
             j = slot_holding(right_order, b)
             state = first_value(j, b)
-            halves = []
-            for h in range(2):
-                part = lax.dot_general(
-                    state,
-                    rbuf[j, h].reshape(kdev * width, width),
-                    NT,
-                    preferred_element_type=jnp.float32,
-                ).astype(jnp.bfloat16)
-                halves += [part[:, k * width : (k + 1) * width] for k in range(kdev)]
+            part = jnp.dot(state, lanes(rbuf, j), preferred_element_type=jnp.float32)
+            part = part.astype(jnp.bfloat16)
+            halves = [part[:, k * width : (k + 1) * width] for k in range(2 * kdev)]
             inner.append(jnp.concatenate(halves, axis=0))
         both = jnp.dot(
             left_wide, jnp.concatenate(inner, axis=1), preferred_element_type=jnp.float32
@@ -426,6 +423,7 @@
         scratch_shapes=[
             pltpu.VMEM((slots,) + block, bf16),
             *[pltpu.SMEM(table.shape, jnp.int32) for table in tables],
+            pltpu.VMEM((kdev,) + block, bf16),
             dma((9,)),
             pltpu.VMEM((slots, 2, kdev) + block, bf16),
             pltpu.VMEM((2, kdev) + block, bf16),

time: 36.3 us -> 36.3 us (level)
  no operation moved by 1% of the time
where the time goes in v5:
time: 36.3 us; the launch traced here: 36.1 us
  Pallas kernels  35.5 us (98%)
  between operations  0.64 us (2%)
    pallas_call x1, Pallas kernels, by_kernel(): pl.pallas_call(functools.partial(kernel, nz, nl), out_shape=shapes, in_sp...  33.5 us
    pallas_call x1, Pallas kernels, by_kernel(): pl.pallas_call(functools.partial(hand_over, parts), out_shape=shapes, in_...  2.01 us

profile of v5, /device:TPU:0, one launch (start us, length us, event | category | flops | bytes accessed | tf_op | source)
XLA Modules:
  0.0 36.1 jit_solution(11292319611922704158)
XLA Ops:
  0.6 33.5 %shard_map.104 = (bf16[1,16,128,128]{3,2,1,0:T(8,128)(2,1)}, bf16[1,8,128,128]{3,2,1,0:T(8,128)(2,1)}) custom-call(bf16[1,16,128,128]{3,2,1,0:T(8,128)(2,1)} %psi_hbm.1, bf16[2,1,128,128]{3,2,1,0:T(8,128)(2,1)} %left_hbm.1, bf16[2,1,128,128]{3,2,1,0:T(8,128)(2,1)} %right_hbm.1, s32[16]{0:T(128)} %left_order_hbm.1, s32[16]{0:T(128)} %right_order_hbm.1, ...), custom_call_target="tpu_custom_call" | custom-call | flops 805306368 | bytes 4194304 | tf_op jit(solution)/shard_map/pallas_call | solution.py:418
  34.1 2.0 %shard_map.105 = (bf16[1,16,128,128]{3,2,1,0:T(8,128)(2,1)}, bf16[1,8,128,128]{3,2,1,0:T(8,128)(2,1)}) custom-call(bf16[1,16,128,128]{3,2,1,0:T(8,128)(2,1)} %get-tuple-element.4.first_in, bf16[1,8,128,128]{3,2,1,0:T(8,128)(2,1)} %get-tuple-element.5.second_in), custom_call_target="tpu_custom_call" | custom-call | tf_op jit(solution)/shard_map/pallas_call | solution.py:461

commit v6 on v5

--- a/solution.py
+++ b/solution.py
@@ -134,6 +134,7 @@
     to_y = {"ops": op}
     to_x = {"lsec": xp}
     to_c = {"lsec": cp}
+    to_d = {"lsec": xp, "ops": op}
     sent = []
 
     def send(src, dst, send_sem, recv_sem, where):
@@ -180,11 +181,12 @@
                     device_id={"lsec": (l + t) % nl, "rsec": (z + s) % nz},
                     device_id_type=MESH,
                 )
-    pl.semaphore_signal(barrier, inc=1, device_id=to_y, device_id_type=MESH)
+    for where in (to_y, to_d):
+        pl.semaphore_signal(barrier, inc=1, device_id=where, device_id_type=MESH)
     loads[0].wait()
     for k in range(kdev):
         rbuf[me, o, k] = right_own[k].astype(jnp.float32).T.astype(jnp.bfloat16)
-    pl.semaphore_wait(barrier, slots)
+    pl.semaphore_wait(barrier, slots + 1)
 
     def slot_of(lane, s):
         return lane * nz + (z + s) % nz
@@ -196,24 +198,32 @@
         send(piece, piece, ysend.at[s], yrecv.at[s], to_y)
         send(piece, piece, xsend.at[s], xrecv.at[s], to_x)
 
+        if s == nz - 1:
+            send(piece, piece, dsend.at[0, s], drecv.at[0, s], to_d)
+
+    def cut(s):
+        return 0 if s == 1 else 1
+
     def stage_two(s):
         mine, theirs = slot_of(l, s), slot_of(xp, s)
         arrive(rbuf.at[theirs, o], xrecv.at[s])
-        cut = 0 if s == 1 else 1
-        if cut:
+        if s < nz - 1 and cut(s):
             half = rbuf.at[theirs, o, 0]
             send(half, half, dsend.at[0, s], drecv.at[0, s], to_y)
         arrive(rbuf.at[mine, op], yrecv.at[s])
-        rest = rbuf.at[mine, op, pl.ds(cut, kdev - cut)]
-        send(rest, rest, dsend.at[1, s], drecv.at[1, s], to_x)
+        if s < nz - 1:
+            rest = rbuf.at[mine, op, pl.ds(cut(s), kdev - cut(s))]
+            send(rest, rest, dsend.at[1, s], drecv.at[1, s], to_x)
         send(rbuf.at[mine], rbuf.at[mine], csend.at[0, s], crecv.at[0, s], to_c)
 
     def stage_three(s):
         theirs = slot_of(xp, s)
-        cut = 0 if s == 1 else 1
-        if cut:
-            arrive(rbuf.at[theirs, op, 0], drecv.at[0, s])
-        arrive(rbuf.at[theirs, op, pl.ds(cut, kdev - cut)], drecv.at[1, s])
+        if s == nz - 1:
+            arrive(rbuf.at[theirs, op], drecv.at[0, s])
+        else:
+            if cut(s):
+                arrive(rbuf.at[theirs, op, 0], drecv.at[0, s])
+            arrive(rbuf.at[theirs, op, pl.ds(cut(s), kdev - cut(s))], drecv.at[1, s])
         send(rbuf.at[theirs], rbuf.at[theirs], csend.at[1, s], crecv.at[1, s], to_c)
 
     def stage_four(s):
@@ -274,8 +284,8 @@
         sigma[j] = first_value(j, right_order[j])
 
     def direct(plane, s):
-        if s == 0:
-            return list(range(1, nl))
+        if s == 0 or s == nz - 1:
+            return list(range(0 if s else 1, nl))
         return [2 * u + (plane + s) % 2 for u in range(nl // 2)]
 
     def source_of(s, t):
@@ -317,24 +327,27 @@
     lax.fori_loop(0, slots, find, 0)
     quarter = slots // 4
     lax.fori_loop(0, quarter, terms_pair, 0, unroll=2)
-    for step in range(2, nz + 3):
+    for step in range(2, nz + 2):
         if step < nz:
             stage_one(step)
-        if 1 <= step - 1 < nz:
+        if step - 1 < nz:
             stage_two(step - 1)
-        if 0 <= step - 2 < nz:
+        if step - 2 < nz - 1:
             stage_three(step - 2)
+        if step == nz:
+            stage_three(nz - 1)
         if step == 2:
             lax.fori_loop(quarter, 2 * quarter, terms_pair, 0, unroll=2)
-        if 0 <= step - 3 < nz:
+        if 0 <= step - 3:
             stage_four(step - 3)
             first_direct(step - 3)
-        if 0 < step - 5 < nz - 2:
-            relay(step - 5)
+    stage_four(nz - 1)
+    first_direct(nz - 1)
+    for s in range(1, nz - 2):
+        relay(s)
 
     first_block(me)
     landed[me] = sigma[me]
-    relay(nz - 2)
 
     count = second_ref.shape[1]
     left_wide = jnp.concatenate([lbuf[h, k] for h in range(2) for k in range(kdev)], axis=1)
@@ -359,14 +372,15 @@
         return carry
 
     lax.fori_loop(0, count // 4, second_pair, 0)
-    relay(nz - 1)
+    relay(nz - 2)
     lax.fori_loop(count // 4, count // 2, second_pair, 0)
     out_second = pltpu.make_async_copy(second, second_ref.at[0], osem.at[0])
     out_second.start()
 
-    for u, t in enumerate(direct(o, 0)):
-        arrive(landed.at[source_of(0, t)], srecv.at[0, u])
-    for s in range(1, nz):
+    for s in (0, nz - 1):
+        for u, t in enumerate(direct(o, s)):
+            arrive(landed.at[source_of(s, t)], srecv.at[s, u])
+    for s in range(1, nz - 1):
         for u in range(nl // 2):
             arrive(landed.at[source_of(s, direct(op, s)[u])], frecv.at[s, u])
 

time: 36.3 us -> 38.1 us (1.050)
  the two profiles are of different devices: /device:TPU:0 before, /device:TPU:18 now
where the time goes in v6:
time: 38.1 us; the launch traced here: 38 us
  Pallas kernels  37.3 us (98%)
  between operations  0.64 us (2%)
    pallas_call x1, Pallas kernels, by_kernel(): pl.pallas_call(functools.partial(kernel, nz, nl), out_shape=shapes, in_sp...  35.3 us
    pallas_call x1, Pallas kernels, by_kernel(): pl.pallas_call(functools.partial(hand_over, parts), out_shape=shapes, in_...  2.01 us

profile of v6, /device:TPU:18, one launch (start us, length us, event | category | flops | bytes accessed | tf_op | source)
XLA Modules:
  0.0 38.0 jit_solution(2063245055788335996)
XLA Ops:
  0.6 35.3 %shard_map.104 = (bf16[1,16,128,128]{3,2,1,0:T(8,128)(2,1)}, bf16[1,8,128,128]{3,2,1,0:T(8,128)(2,1)}) custom-call(bf16[1,16,128,128]{3,2,1,0:T(8,128)(2,1)} %psi_hbm.1, bf16[2,1,128,128]{3,2,1,0:T(8,128)(2,1)} %left_hbm.1, bf16[2,1,128,128]{3,2,1,0:T(8,128)(2,1)} %right_hbm.1, s32[16]{0:T(128)} %left_order_hbm.1, s32[16]{0:T(128)} %right_order_hbm.1, ...), custom_call_target="tpu_custom_call" | custom-call | flops 805306368 | bytes 4194304 | tf_op jit(solution)/shard_map/pallas_call | solution.py:432
  36.0 2.0 %shard_map.105 = (bf16[1,16,128,128]{3,2,1,0:T(8,128)(2,1)}, bf16[1,8,128,128]{3,2,1,0:T(8,128)(2,1)}) custom-call(bf16[1,16,128,128]{3,2,1,0:T(8,128)(2,1)} %get-tuple-element.4.first_in, bf16[1,8,128,128]{3,2,1,0:T(8,128)(2,1)} %get-tuple-element.5.second_in), custom_call_target="tpu_custom_call" | custom-call | tf_op jit(solution)/shard_map/pallas_call | solution.py:475

commit v7 on v5

--- a/solution.py
+++ b/solution.py
@@ -186,13 +186,18 @@
         rbuf[me, o, k] = right_own[k].astype(jnp.float32).T.astype(jnp.bfloat16)
     pl.semaphore_wait(barrier, slots)
 
+    pair = z + 1 - 2 * (z % 2)
+    group = [z, pair, (z + 2) % nz, (pair + 2) % nz]
+
     def slot_of(lane, s):
-        return lane * nz + (z + s) % nz
+        return lane * nz + group[s]
 
     def stage_one(s):
         piece = rbuf.at[slot_of(l, s), o]
         if s:
             arrive(piece, zrecv.at[s])
+        if s == 2:
+            send(piece, piece, zsend.at[3], zrecv.at[3], {"rsec": pair})
         send(piece, piece, ysend.at[s], yrecv.at[s], to_y)
         send(piece, piece, xsend.at[s], xrecv.at[s], to_x)
 
@@ -220,9 +225,9 @@
         arrive(rbuf.at[slot_of(cp, s)], crecv.at[0, s])
         arrive(rbuf.at[slot_of((cp + 2) % nl, s)], crecv.at[1, s])
 
-    for s in range(1, nz):
+    for s in (1, 2):
         piece = rbuf.at[me, o]
-        send(piece, piece, zsend.at[s], zrecv.at[s], {"rsec": (z + nz - s) % nz})
+        send(piece, piece, zsend.at[s], zrecv.at[s], {"rsec": group[s]})
     stage_one(0)
     loads[1].wait()
     send(lbuf.at[o], lbuf.at[o], lsend, lrecv, to_y)
@@ -279,7 +284,7 @@
         return [2 * u + (plane + s) % 2 for u in range(nl // 2)]
 
     def source_of(s, t):
-        return ((l + nl - t) % nl) * nz + (z + nz - s) % nz
+        return ((l + nl - t) % nl) * nz + group[s]
 
     def first_direct(s):
         targets = [(l + t) % nl for t in direct(o, s)]
@@ -291,7 +296,7 @@
                 landed.at[me],
                 ssend.at[s, u],
                 srecv.at[s, u],
-                {"lsec": there, "rsec": (z + s) % nz},
+                {"lsec": there, "rsec": group[s]},
             )
 
     def relay(s):
@@ -477,7 +482,7 @@
 
     def on_device(psi, left_ops, right_ops, *tables):
         gathered = no * nl * nz * left_ops.size * left_ops.dtype.itemsize
-        if no == 2 and nl == 4 and nz > 2 and left_ops.shape[0] > 1 and 3 * gathered <= VMEM_BUDGET:
+        if no == 2 and nl == 4 and nz == 4 and left_ops.shape[0] > 1 and 3 * gathered <= VMEM_BUDGET:
             return by_kernel(nz, nl, psi, left_ops, right_ops, *tables)
         return by_collectives(psi, left_ops, right_ops, *tables)
 

time: 36.3 us -> 36.5 us (level)
  the two profiles are of different devices: /device:TPU:0 before, /device:TPU:1 now
where the time goes in v7:
time: 36.5 us; the launch traced here: 36.3 us
  Pallas kernels  35.7 us (98%)
  between operations  0.64 us (2%)
    pallas_call x1, Pallas kernels, by_kernel(): pl.pallas_call(functools.partial(kernel, nz, nl), out_shape=shapes, in_sp...  33.7 us
    pallas_call x1, Pallas kernels, by_kernel(): pl.pallas_call(functools.partial(hand_over, parts), out_shape=shapes, in_...  2.01 us

profile of v7, /device:TPU:1, one launch (start us, length us, event | category | flops | bytes accessed | tf_op | source)
XLA Modules:
  0.0 36.3 jit_solution(8118412097845456124)
XLA Ops:
  0.6 33.7 %shard_map.104 = (bf16[1,16,128,128]{3,2,1,0:T(8,128)(2,1)}, bf16[1,8,128,128]{3,2,1,0:T(8,128)(2,1)}) custom-call(bf16[1,16,128,128]{3,2,1,0:T(8,128)(2,1)} %psi_hbm.1, bf16[2,1,128,128]{3,2,1,0:T(8,128)(2,1)} %left_hbm.1, bf16[2,1,128,128]{3,2,1,0:T(8,128)(2,1)} %right_hbm.1, s32[16]{0:T(128)} %left_order_hbm.1, s32[16]{0:T(128)} %right_order_hbm.1, ...), custom_call_target="tpu_custom_call" | custom-call | flops 805306368 | bytes 4194304 | tf_op jit(solution)/shard_map/pallas_call | solution.py:423
  34.3 2.0 %shard_map.105 = (bf16[1,16,128,128]{3,2,1,0:T(8,128)(2,1)}, bf16[1,8,128,128]{3,2,1,0:T(8,128)(2,1)}) custom-call(bf16[1,16,128,128]{3,2,1,0:T(8,128)(2,1)} %get-tuple-element.4.first_in, bf16[1,8,128,128]{3,2,1,0:T(8,128)(2,1)} %get-tuple-element.5.second_in), custom_call_target="tpu_custom_call" | custom-call | tf_op jit(solution)/shard_map/pallas_call | solution.py:466

commit v8 on v7

--- a/solution.py
+++ b/solution.py
@@ -244,24 +244,25 @@
         used = jnp.where(jnp.abs(my_qn - right_qn[b]) <= SPREAD, right_dims[b], 0)
         return jnp.where(rows_used & (cols < used), value, 0.0).astype(jnp.bfloat16)
 
-    def start_pair(pair, carry):
+    def left_terms(h, two):
+        both = jnp.dot(
+            lbuf[h].reshape(kdev * width, width), start[two], preferred_element_type=jnp.float32
+        )
+        both = both.astype(jnp.bfloat16).reshape(kdev, width, 2 * width)
+        terms[2 * two, h] = both[:, :, :width]
+        terms[2 * two + 1, h] = both[:, :, width:]
+
+    def own_terms(two, carry):
         blocks = []
-        for j in (2 * pair, 2 * pair + 1):
+        for j in (2 * two, 2 * two + 1):
             b = right_order[j]
             blocks.append(masked(psi[b].astype(jnp.float32), b))
-        start[pair] = jnp.concatenate(blocks, axis=1)
+        start[two] = jnp.concatenate(blocks, axis=1)
+        left_terms(o, two)
         return carry
 
-    def terms_pair(pair, carry):
-        for h in range(2):
-            both = jnp.dot(
-                lbuf[h].reshape(kdev * width, width),
-                start[pair],
-                preferred_element_type=jnp.float32,
-            )
-            both = both.astype(jnp.bfloat16).reshape(kdev, width, 2 * width)
-            terms[2 * pair, h] = both[:, :, :width]
-            terms[2 * pair + 1, h] = both[:, :, width:]
+    def other_terms(two, carry):
+        left_terms(op, two)
         return carry
 
     def lanes(ref, j):
@@ -305,10 +306,9 @@
             arrive(block, srecv.at[s, u])
             send(block, block, fsend.at[s, u], frecv.at[s, u], to_y)
 
-    lax.fori_loop(0, slots // 2, start_pair, 0, unroll=2)
+    lax.fori_loop(0, slots // 2, own_terms, 0, unroll=2)
     stage_one(1)
     stage_two(0)
-    arrive(lbuf.at[op], lrecv)
     def slot_holding(order, wanted):
         found = jnp.int32(0)
         for j in range(slots):
@@ -319,9 +319,6 @@
         inverse_left[a] = slot_holding(left_order, a)
         return carry
 
-    lax.fori_loop(0, slots, find, 0)
-    quarter = slots // 4
-    lax.fori_loop(0, quarter, terms_pair, 0, unroll=2)
     for step in range(2, nz + 3):
         if step < nz:
             stage_one(step)
@@ -330,7 +327,9 @@
         if 0 <= step - 2 < nz:
             stage_three(step - 2)
         if step == 2:
-            lax.fori_loop(quarter, 2 * quarter, terms_pair, 0, unroll=2)
+            arrive(lbuf.at[op], lrecv)
+            lax.fori_loop(0, slots // 2, other_terms, 0, unroll=2)
+            lax.fori_loop(0, slots, find, 0)
         if 0 <= step - 3 < nz:
             stage_four(step - 3)
             first_direct(step - 3)

time: 36.5 us -> 36.1 us (0.989)
  the two profiles are of different devices: /device:TPU:1 before, /device:TPU:0 now
where the time goes in v8:
time: 36.1 us; the launch traced here: 35.9 us
  Pallas kernels  35.3 us (98%)
  between operations  0.64 us (2%)
    pallas_call x1, Pallas kernels, by_kernel(): pl.pallas_call(functools.partial(kernel, nz, nl), out_shape=shapes, in_sp...  33.3 us
    pallas_call x1, Pallas kernels, by_kernel(): pl.pallas_call(functools.partial(hand_over, parts), out_shape=shapes, in_...  2.01 us

profile of v8, /device:TPU:0, one launch (start us, length us, event | category | flops | bytes accessed | tf_op | source)
XLA Modules:
  0.0 35.9 jit_solution(11323848044611714147)
XLA Ops:
  0.6 33.3 %shard_map.104 = (bf16[1,16,128,128]{3,2,1,0:T(8,128)(2,1)}, bf16[1,8,128,128]{3,2,1,0:T(8,128)(2,1)}) custom-call(bf16[1,16,128,128]{3,2,1,0:T(8,128)(2,1)} %psi_hbm.1, bf16[2,1,128,128]{3,2,1,0:T(8,128)(2,1)} %left_hbm.1, bf16[2,1,128,128]{3,2,1,0:T(8,128)(2,1)} %right_hbm.1, s32[16]{0:T(128)} %left_order_hbm.1, s32[16]{0:T(128)} %right_order_hbm.1, ...), custom_call_target="tpu_custom_call" | custom-call | flops 805306368 | bytes 4194304 | tf_op jit(solution)/shard_map/pallas_call | solution.py:422
  33.9 2.0 %shard_map.105 = (bf16[1,16,128,128]{3,2,1,0:T(8,128)(2,1)}, bf16[1,8,128,128]{3,2,1,0:T(8,128)(2,1)}) custom-call(bf16[1,16,128,128]{3,2,1,0:T(8,128)(2,1)} %get-tuple-element.4.first_in, bf16[1,8,128,128]{3,2,1,0:T(8,128)(2,1)} %get-tuple-element.5.second_in), custom_call_target="tpu_custom_call" | custom-call | tf_op jit(solution)/shard_map/pallas_call | solution.py:465

commit v9 on v8

--- a/solution.py
+++ b/solution.py
@@ -362,9 +362,8 @@
             )
         return carry
 
-    lax.fori_loop(0, count // 4, second_pair, 0)
     relay(nz - 1)
-    lax.fori_loop(count // 4, count // 2, second_pair, 0)
+    lax.fori_loop(0, count // 2, second_pair, 0)
     out_second = pltpu.make_async_copy(second, second_ref.at[0], osem.at[0])
     out_second.start()
 

time: 36.1 us -> 36.1 us (level)
  no operation moved by 1% of the time
where the time goes in v9:
time: 36.1 us; the launch traced here: 35.9 us
  Pallas kernels  35.3 us (98%)
  between operations  0.64 us (2%)
    pallas_call x1, Pallas kernels, by_kernel(): pl.pallas_call(functools.partial(kernel, nz, nl), out_shape=shapes, in_sp...  33.3 us
    pallas_call x1, Pallas kernels, by_kernel(): pl.pallas_call(functools.partial(hand_over, parts), out_shape=shapes, in_...  2.01 us

profile of v9, /device:TPU:0, one launch (start us, length us, event | category | flops | bytes accessed | tf_op | source)
XLA Modules:
  0.0 35.9 jit_solution(17217160803962380550)
XLA Ops:
  0.6 33.3 %shard_map.104 = (bf16[1,16,128,128]{3,2,1,0:T(8,128)(2,1)}, bf16[1,8,128,128]{3,2,1,0:T(8,128)(2,1)}) custom-call(bf16[1,16,128,128]{3,2,1,0:T(8,128)(2,1)} %psi_hbm.1, bf16[2,1,128,128]{3,2,1,0:T(8,128)(2,1)} %left_hbm.1, bf16[2,1,128,128]{3,2,1,0:T(8,128)(2,1)} %right_hbm.1, s32[16]{0:T(128)} %left_order_hbm.1, s32[16]{0:T(128)} %right_order_hbm.1, ...), custom_call_target="tpu_custom_call" | custom-call | flops 805306368 | bytes 4194304 | tf_op jit(solution)/shard_map/pallas_call | solution.py:421
  33.9 2.0 %shard_map.105 = (bf16[1,16,128,128]{3,2,1,0:T(8,128)(2,1)}, bf16[1,8,128,128]{3,2,1,0:T(8,128)(2,1)}) custom-call(bf16[1,16,128,128]{3,2,1,0:T(8,128)(2,1)} %get-tuple-element.4.first_in, bf16[1,8,128,128]{3,2,1,0:T(8,128)(2,1)} %get-tuple-element.5.second_in), custom_call_target="tpu_custom_call" | custom-call | tf_op jit(solution)/shard_map/pallas_call | solution.py:464
